TPU v7x, 512 devices: a whole 4x8x8 slice. The times are simulated.
512 devices in a mesh: group: 16 (over x, y_hi, core), sub: 32 (over y_lo, z).
Axes of the slice: x: 4, y: 8 (y_hi: 2, y_lo: 4; y = y_hi * 4 + y_lo), z: 8, core: 2. Of those that a mesh axis runs over, the one named last changes fastest.
Arguments:
- fine_residual: bfloat16 [2, 12, 4, 524288], P(None, None, None, ('group', 'sub')), may hold values from -6 to 6
- null_vectors: bfloat16 [2, 12, 32, 524288], P(None, None, None, ('group', 'sub')), may hold values from -0.15625 to 0.15625
- agg_map: int32 [512, 1024], P(('group', 'sub')), may hold values from 0 to 1023, each once within a row
- block_owner: int32 [16], replicated, may hold values from 0 to 15, each once
- coarse_links: bfloat16 [9, 16, 32, 2, 2, 64, 64], P(None, 'group', 'sub'), may hold values from -0.125 to 0.125
Outputs:
- coarse_solution: float32 [16, 32, 2, 2, 4, 64], P('group', 'sub')
- correction: bfloat16 [2, 12, 4, 524288], P(None, None, None, ('group', 'sub'))
Inputs may be any that keep to these rules, and one draw needn't show every extreme that they name: `agg_map`: each row lists every local fine site of its device exactly once. `block_owner`: each group holds a different coarse block.
All inputs are finite; a program needn't handle non-finite values.
Results may differ from a plain program's by a relative error of at most 0.015.
Values may be sent and summed in bfloat16 or wider, within the bound.
A program may use at most 64 MiB of HBM per device.

v0:
```python
import jax
import jax.numpy as jnp
from jax import lax
from jax.sharding import PartitionSpec as P

SPIN_COLOR = 12
NULLV = 32
AGG = 256
COARSE_STEPS = 4
CDOF = 64


def padded_2(cells, sides, width):
    for axis, dim in sides:
        count = lax.axis_size(axis)
        head = lax.slice_in_dim(cells, 0, width, axis=dim)
        tail = lax.slice_in_dim(cells, cells.shape[dim] - width, cells.shape[dim], axis=dim)
        cells = jnp.concatenate(
            [
                lax.ppermute(tail, axis, [(i, (i + 1) % count) for i in range(count)]),
                cells,
                lax.ppermute(head, axis, [((i + 1) % count, i) for i in range(count)]),
            ],
            axis=dim,
        )
    return cells


def neighbour(field, stride, axis_number):
    length = field.shape[axis_number]
    widths = [(0, 0)] * field.ndim
    widths[axis_number] = (1, 1)
    padded = jnp.pad(field, widths)
    return lax.slice_in_dim(padded, 1 + stride, 1 + stride + length, axis=axis_number)


def hopping(blocks, centre, ahead_x, behind_x, ahead_t, behind_t):
    shifted = (
        centre,
        ahead_x,
        behind_x,
        ahead_t,
        behind_t,
        neighbour(centre, 1, 2),
        neighbour(centre, -1, 2),
        neighbour(centre, 1, 3),
        neighbour(centre, -1, 3),
    )
    summed = jnp.zeros(centre.shape, jnp.float32)
    for direction in range(9):
        summed = summed + jnp.einsum(
            "xtyzij,xtyzrj->xtyzri",
            blocks[direction],
            shifted[direction],
            preferred_element_type=jnp.float32,
        )
    return summed


def on_device(fine_residual, null_vectors, agg_map, block_owner, coarse_links):
    site_order = agg_map[0]
    num_rhs = fine_residual.shape[2]
    num_sites = site_order.shape[0]
    num_aggs = num_sites // AGG
    site_ids = jnp.arange(num_sites, dtype=jnp.int32)
    mapping = (site_ids[:, None] == site_order[None, :]).astype(jnp.bfloat16)
    fine_agg = jnp.dot(
        fine_residual.reshape(-1, num_sites), mapping, preferred_element_type=jnp.float32
    ).astype(jnp.bfloat16)
    fine_agg = fine_agg.reshape(2, SPIN_COLOR, num_rhs, num_aggs, AGG)
    null_agg = jnp.dot(
        null_vectors.reshape(-1, num_sites), mapping, preferred_element_type=jnp.float32
    ).astype(jnp.bfloat16)
    null_agg = null_agg.reshape(2, SPIN_COLOR, NULLV, num_aggs, AGG)
    form = "fcas,fras->arc"
    real_part = jnp.einsum(
        form, null_agg[0], fine_agg[0], preferred_element_type=jnp.float32
    ) + jnp.einsum(form, null_agg[1], fine_agg[1], preferred_element_type=jnp.float32)
    imag_part = jnp.einsum(
        form, null_agg[0], fine_agg[1], preferred_element_type=jnp.float32
    ) - jnp.einsum(form, null_agg[1], fine_agg[0], preferred_element_type=jnp.float32)
    local_shape = coarse_links.shape[2:5]
    restricted = jnp.concatenate([real_part, imag_part], axis=-1).reshape(
        local_shape + (num_rhs, CDOF)
    )
    group_here = lax.axis_index("group")
    num_groups = lax.axis_size("group")
    owner_here = block_owner[group_here]
    group_ids = jnp.arange(num_groups, dtype=jnp.int32)
    pieces = lax.all_gather(restricted[None], "group", axis=0, tiled=True)
    placing = (block_owner[None, :] == group_ids[:, None]).astype(jnp.float32)
    coarse_rhs = jnp.tensordot(placing, pieces, axes=1, precision=lax.Precision.HIGHEST)
    blocks = lax.all_gather(coarse_links, "group", axis=1, tiled=True)
    iterate = coarse_rhs
    for step in range(COARSE_STEPS):
        lowered = iterate.astype(jnp.bfloat16)
        padded = padded_2(lowered, (("sub", 1),), 1)
        iterate = coarse_rhs - hopping(
            blocks,
            lowered,
            jnp.roll(lowered, -1, 0),
            jnp.roll(lowered, 1, 0),
            padded[:, 2:],
            padded[:, :-2],
        )
    solution_here = lax.dynamic_slice_in_dim(iterate, group_here, 1, 0)
    own_block = lax.dynamic_slice_in_dim(iterate, owner_here, 1, 0)
    rounded = own_block.astype(jnp.bfloat16).reshape(num_aggs, num_rhs, CDOF)
    part_re = rounded[..., :NULLV]
    part_im = rounded[..., NULLV:]
    back = "fcas,arc->fras"
    corr_re = jnp.einsum(
        back, null_agg[0], part_re, preferred_element_type=jnp.float32
    ) - jnp.einsum(back, null_agg[1], part_im, preferred_element_type=jnp.float32)
    corr_im = jnp.einsum(
        back, null_agg[0], part_im, preferred_element_type=jnp.float32
    ) + jnp.einsum(back, null_agg[1], part_re, preferred_element_type=jnp.float32)
    stacked = jnp.stack([corr_re, corr_im]).astype(jnp.bfloat16).reshape(-1, num_sites)
    placed = lax.dot_general(
        stacked, mapping, (((1,), (1,)), ((), ())), preferred_element_type=jnp.float32
    )
    return (solution_here, placed.astype(jnp.bfloat16).reshape(2, SPIN_COLOR, num_rhs, num_sites))


def solution(mesh):
    in_specs = (
        P(None, None, None, ("group", "sub")),
        P(None, None, None, ("group", "sub")),
        P(("group", "sub"), None),
        P(),
        P(None, "group", "sub", None, None, None, None),
    )
    out_specs = (P("group", "sub", None, None, None, None), P(None, None, None, ("group", "sub")))
    return jax.shard_map(
        on_device, mesh=mesh, in_specs=in_specs, out_specs=out_specs, check_vma=False
    )
```

profile of v0, /device:TPU:1, one launch (start us, length us, event | category | flops | bytes accessed | tf_op | source)
XLA Modules:
  0.0 211.7 jit_solution(16012891550462582602)
XLA Ops:
  7.2 0.7 all-gather.2.cloned.1.call-update
  7.9 0.7 copy-done
  8.6 2.6 %fusion.11 = bf16[768,1024]{0,1:T(8,128)(2,1)S(1)} fusion(bf16[768,1024]{1,0:T(8,128)(2,1)S(1)} %bitcast.211, s32[1024]{0:T(1024)} %bitcast.239), kind=kOutput, calls=%fused_computation.9 | convolution fusion | flops 1613496320 | bytes 3149824 | tf_op jit(solution)/shard_map/dot_general | solution.py:71
  11.2 1.0 fusion.138
  12.6 0.6 squeeze.11
  13.2 0.8 fusion.16
  14.1 2.3 %copy.201 = bf16[384,1024]{1,0:T(8,128)(2,1)} copy(bf16[384,1024]{0,1:T(8,128)(2,1)} %get-tuple-element.2) | data formatting | bytes 1572864 | tf_op jit(solution)/shard_map/slice | solution.py:78
  16.4 1.9 squeeze.13
  19.4 0.3 fusion.22
  19.8 36.8 %all_gather.6 = f32[16,1,2,2,4,64]{5,4,3,2,1,0:T(4,128)S(1)} all-gather(f32[1,1,2,2,4,64]{5,4,3,2,1,0:T(4,128)S(1)} %bitcast.237), channel_id=1, replica_groups=mesh['group'=16,'sub'=32] {'group'}, dimensions={0}, use_global_device_ids=true | all-gather | bytes 69632 | tf_op jit(solution)/shard_map/all_gather | solution.py:90
  56.9 3.3 %collective-permute-start.1 = (bf16[16,1,2,2,4,64]{5,0,4,3,2,1:T(8,128)(2,1)S(1)}, bf16[16,1,2,2,4,64]{5,0,4,3,2,1:T(8,128)(2,1)}, u32[]{:S(2)}, u32[]{:S(2)}) collective-permute-start(bf16[16,1,2,2,4,64]{5,0,4,3,2,1:T(8,128)(2,1)S(1)} %bitcast.212), channel_id=1, source_target_pairs={{0,1},{1,2},{2,3},{3,4},{4,5},{5,6},{6,7},{7,8},{8,9},{9,10},{10,1... | collective-permute-start | bytes 98312 | tf_op jit(solution)/shard_map/ppermute | solution.py:20
  60.1 6.9 %collective-permute-start = (bf16[16,1,2,2,4,64]{5,0,4,3,2,1:T(8,128)(2,1)S(1)}, bf16[16,1,2,2,4,64]{5,0,4,3,2,1:T(8,128)(2,1)}, u32[]{:S(2)}, u32[]{:S(2)}) collective-permute-start(bf16[16,1,2,2,4,64]{5,0,4,3,2,1:T(8,128)(2,1)S(1)} %bitcast.213), channel_id=1, source_target_pairs={{1,0},{2,1},{3,2},{4,3},{5,4},{6,5},{7,6},{8,7},{9,8},{10,9},{11,1... | collective-permute-start | bytes 98312 | tf_op jit(solution)/shard_map/ppermute | solution.py:22
  67.0 0.6 dynamic_slice.8
  69.7 0.7 fusion.83
  70.4 66.8 %all-gather.2.cloned.1.call-done = bf16[9,16,1,2,2,64,64]{6,5,4,3,1,2,0:T(8,128)(2,1)} async-done(((bf16[9,1,1,2,2,64,64]{6,5,4,3,1,2,0:T(8,128)(2,1)}), bf16[9,16,1,2,2,64,64]{6,5,4,3,1,2,0:T(8,128)(2,1)}) %all-gather.2.cloned.1.call-update) | async-done | bytes 4718608 | tf_op jit(solution)/shard_map/all_gather | solution.py:93
  137.2 2.0 fusion.26
  139.2 2.4 %fusion.58 = f32[16,2,2,4,64]{4,3,2,1,0:T(4,128)S(1)} fusion(bf16[9,16,1,2,2,64,64]{6,5,4,3,1,2,0:T(8,128)(2,1)} %all-gather.2.cloned.1.call-done, bf16[16,2,2,4,64]{4,0,3,2,1:T(8,128)(2,1)} %get-tuple-element.36), kind=kOutput, calls=%fused_computation.69 | convolution fusion | flops 2097152 | bytes 1179648 | tf_op jit(solution)/shard_map/xtyzij,xtyzrj->xtyzri/dot_general | solution.py:51
  141.6 1.9 fusion.54
  143.5 1.9 fusion.50
  145.4 1.9 fusion.46
  147.3 1.9 fusion.42
  149.3 1.9 fusion.38
  151.2 1.9 fusion.34
  153.1 0.7 fusion.30
  153.7 0.4 fusion.77
  154.1 3.3 %collective-permute-start.3 = (bf16[16,1,2,2,4,64]{5,0,4,3,2,1:T(8,128)(2,1)S(1)}, bf16[16,1,2,2,4,64]{5,0,4,3,2,1:T(8,128)(2,1)S(1)}, u32[]{:S(2)}, u32[]{:S(2)}) collective-permute-start(bf16[16,1,2,2,4,64]{5,0,4,3,2,1:T(8,128)(2,1)S(1)} %bitcast.216), channel_id=1, source_target_pairs={{0,1},{1,2},{2,3},{3,4},{4,5},{5,6},{6,7},{7,8},{8,9},{9,10},{10,1... | collective-permute-start | bytes 98312 | tf_op jit(solution)/shard_map/ppermute | solution.py:20
  157.4 6.1 %collective-permute-start.2 = (bf16[16,1,2,2,4,64]{5,0,4,3,2,1:T(8,128)(2,1)S(1)}, bf16[16,1,2,2,4,64]{5,0,4,3,2,1:T(8,128)(2,1)S(1)}, u32[]{:S(2)}, u32[]{:S(2)}) collective-permute-start(bf16[16,1,2,2,4,64]{5,0,4,3,2,1:T(8,128)(2,1)S(1)} %bitcast.217), channel_id=1, source_target_pairs={{1,0},{2,1},{3,2},{4,3},{5,4},{6,5},{7,6},{8,7},{9,8},{10,9},{11,1... | collective-permute-start | bytes 98312 | tf_op jit(solution)/shard_map/ppermute | solution.py:22
  163.6 0.6 fusion.25
  164.3 0.7 fusion.57
  164.9 0.7 fusion.53
  165.6 0.7 fusion.49
  166.2 0.7 fusion.45
  166.9 0.7 fusion.33
  167.5 0.7 fusion.29
  168.2 0.7 fusion.41
  168.9 0.7 fusion.37
  169.5 0.4 fusion.75
  169.9 1.9 collective-permute-start.5
  171.9 7.3 %collective-permute-start.4 = (bf16[16,1,2,2,4,64]{5,0,4,3,2,1:T(8,128)(2,1)S(1)}, bf16[16,1,2,2,4,64]{5,0,4,3,2,1:T(8,128)(2,1)S(1)}, u32[]{:S(2)}, u32[]{:S(2)}) collective-permute-start(bf16[16,1,2,2,4,64]{5,0,4,3,2,1:T(8,128)(2,1)S(1)} %bitcast.220), channel_id=1, source_target_pairs={{1,0},{2,1},{3,2},{4,3},{5,4},{6,5},{7,6},{8,7},{9,8},{10,9},{11,1... | collective-permute-start | bytes 98312 | tf_op jit(solution)/shard_map/ppermute | solution.py:22
  179.3 0.6 fusion.24
  179.9 0.7 fusion.56
  180.6 0.7 fusion.52
  181.2 0.7 fusion.48
  181.9 0.7 fusion.44
  182.5 0.7 fusion.32
  183.2 0.7 fusion.28
  183.8 0.7 fusion.40
  184.5 0.7 fusion.36
  185.2 0.4 fusion.73
  185.6 1.9 collective-permute-start.7
  187.5 7.3 %collective-permute-start.6 = (bf16[16,1,2,2,4,64]{5,0,4,3,2,1:T(8,128)(2,1)S(1)}, bf16[16,1,2,2,4,64]{5,0,4,3,2,1:T(8,128)(2,1)S(1)}, u32[]{:S(2)}, u32[]{:S(2)}) collective-permute-start(bf16[16,1,2,2,4,64]{5,0,4,3,2,1:T(8,128)(2,1)S(1)} %bitcast.223), channel_id=1, source_target_pairs={{1,0},{2,1},{3,2},{4,3},{5,4},{6,5},{7,6},{8,7},{9,8},{10,9},{11,1... | collective-permute-start | bytes 98312 | tf_op jit(solution)/shard_map/ppermute | solution.py:22
  194.9 0.6 fusion.23
  195.5 0.7 fusion.55
  196.2 0.7 fusion.51
  196.8 0.7 fusion.47
  197.5 0.7 fusion.43
  198.2 0.7 fusion.31
  198.8 0.7 fusion.27
  199.5 0.7 fusion.39
  200.1 0.7 fusion.35
  200.8 0.4 fusion.71
  201.1 0.6 constant_dynamic-slice_fusion
  203.1 0.9 fusion.15
  204.1 0.8 reshape.369
  (55 shorter events, 3.6 us)
Async XLA Ops:
  7.2 1.4 copy-start
  7.2 130.0 %all-gather.2.cloned.1.call-start = ((), (), s32[]{:S(2)}) async-start(), calls=%async_computation | async-start | bytes 10027008 | tf_op jit(solution)/shard_map/all_gather | solution.py:93
  8.6 4.5 %copy-start.2 = (bf16[2,12,4,1024]{3,2,1,0:T(4,128)(2,1)S(1)}, bf16[2,12,4,1024]{3,2,1,0:T(4,128)(2,1)}, u32[]{:S(2)}) copy-start(bf16[2,12,4,1024]{3,2,1,0:T(4,128)(2,1)} %param.5) | copy-start | bytes 589828
  8.6 4.6 %copy-start.4 = (s32[1,1024]{1,0:T(1,128)S(1)}, s32[1,1024]{1,0:T(1,128)}, u32[]{:S(2)}) copy-start(s32[1,1024]{1,0:T(1,128)} %param.7) | copy-start | bytes 12292
  11.2 45.4 %copy-start.3 = (s32[16]{0:T(128)S(1)}, s32[16]{0:T(128)}, u32[]{:S(2)}) copy-start(s32[16]{0:T(128)} %param.8) | copy-start | bytes 196
  56.9 90.5 %collective-permute-start.1 = (bf16[16,1,2,2,4,64]{5,0,4,3,2,1:T(8,128)(2,1)S(1)}, bf16[16,1,2,2,4,64]{5,0,4,3,2,1:T(8,128)(2,1)}, u32[]{:S(2)}, u32[]{:S(2)}) collective-permute-start(bf16[16,1,2,2,4,64]{5,0,4,3,2,1:T(8,128)(2,1)S(1)} %bitcast.212), channel_id=1, source_target_pairs={{0,1},{1,2},{2,3},{3,4},{4,5},{5,6},{6,7},{7,8},{8,9},{9,10},{10,1... | collective-permute-start | bytes 98312 | tf_op jit(solution)/shard_map/ppermute | solution.py:20
  60.1 89.1 %collective-permute-start = (bf16[16,1,2,2,4,64]{5,0,4,3,2,1:T(8,128)(2,1)S(1)}, bf16[16,1,2,2,4,64]{5,0,4,3,2,1:T(8,128)(2,1)}, u32[]{:S(2)}, u32[]{:S(2)}) collective-permute-start(bf16[16,1,2,2,4,64]{5,0,4,3,2,1:T(8,128)(2,1)S(1)} %bitcast.213), channel_id=1, source_target_pairs={{1,0},{2,1},{3,2},{4,3},{5,4},{6,5},{7,6},{8,7},{9,8},{10,9},{11,1... | collective-permute-start | bytes 98312 | tf_op jit(solution)/shard_map/ppermute | solution.py:22
  137.2 15.8 %copy-start.1 = (bf16[9,16,1,2,2,64,64]{6,5,4,3,1,2,0:T(8,128)(2,1)S(1)}, bf16[9,16,1,2,2,64,64]{6,5,4,3,1,2,0:T(8,128)(2,1)}, u32[]{:S(2)}) copy-start(bf16[9,16,1,2,2,64,64]{6,5,4,3,1,2,0:T(8,128)(2,1)} %all-gather.2.cloned.1.call-done) | copy-start | bytes 14155780
  154.1 14.1 %collective-permute-start.3 = (bf16[16,1,2,2,4,64]{5,0,4,3,2,1:T(8,128)(2,1)S(1)}, bf16[16,1,2,2,4,64]{5,0,4,3,2,1:T(8,128)(2,1)S(1)}, u32[]{:S(2)}, u32[]{:S(2)}) collective-permute-start(bf16[16,1,2,2,4,64]{5,0,4,3,2,1:T(8,128)(2,1)S(1)} %bitcast.216), channel_id=1, source_target_pairs={{0,1},{1,2},{2,3},{3,4},{4,5},{5,6},{6,7},{7,8},{8,9},{9,10},{10,1... | collective-permute-start | bytes 98312 | tf_op jit(solution)/shard_map/ppermute | solution.py:20
  157.4 11.5 %collective-permute-start.2 = (bf16[16,1,2,2,4,64]{5,0,4,3,2,1:T(8,128)(2,1)S(1)}, bf16[16,1,2,2,4,64]{5,0,4,3,2,1:T(8,128)(2,1)S(1)}, u32[]{:S(2)}, u32[]{:S(2)}) collective-permute-start(bf16[16,1,2,2,4,64]{5,0,4,3,2,1:T(8,128)(2,1)S(1)} %bitcast.217), channel_id=1, source_target_pairs={{1,0},{2,1},{3,2},{4,3},{5,4},{6,5},{7,6},{8,7},{9,8},{10,9},{11,1... | collective-permute-start | bytes 98312 | tf_op jit(solution)/shard_map/ppermute | solution.py:22
  169.9 13.9 %collective-permute-start.5 = (bf16[16,1,2,2,4,64]{5,0,4,3,2,1:T(8,128)(2,1)S(1)}, bf16[16,1,2,2,4,64]{5,0,4,3,2,1:T(8,128)(2,1)S(1)}, u32[]{:S(2)}, u32[]{:S(2)}) collective-permute-start(bf16[16,1,2,2,4,64]{5,0,4,3,2,1:T(8,128)(2,1)S(1)} %bitcast.219), channel_id=1, source_target_pairs={{0,1},{1,2},{2,3},{3,4},{4,5},{5,6},{6,7},{7,8},{8,9},{9,10},{10,1... | collective-permute-start | bytes 98312 | tf_op jit(solution)/shard_map/ppermute | solution.py:20
  171.9 12.6 %collective-permute-start.4 = (bf16[16,1,2,2,4,64]{5,0,4,3,2,1:T(8,128)(2,1)S(1)}, bf16[16,1,2,2,4,64]{5,0,4,3,2,1:T(8,128)(2,1)S(1)}, u32[]{:S(2)}, u32[]{:S(2)}) collective-permute-start(bf16[16,1,2,2,4,64]{5,0,4,3,2,1:T(8,128)(2,1)S(1)} %bitcast.220), channel_id=1, source_target_pairs={{1,0},{2,1},{3,2},{4,3},{5,4},{6,5},{7,6},{8,7},{9,8},{10,9},{11,1... | collective-permute-start | bytes 98312 | tf_op jit(solution)/shard_map/ppermute | solution.py:22
  185.6 13.9 %collective-permute-start.7 = (bf16[16,1,2,2,4,64]{5,0,4,3,2,1:T(8,128)(2,1)S(1)}, bf16[16,1,2,2,4,64]{5,0,4,3,2,1:T(8,128)(2,1)S(1)}, u32[]{:S(2)}, u32[]{:S(2)}) collective-permute-start(bf16[16,1,2,2,4,64]{5,0,4,3,2,1:T(8,128)(2,1)S(1)} %bitcast.222), channel_id=1, source_target_pairs={{0,1},{1,2},{2,3},{3,4},{4,5},{5,6},{6,7},{7,8},{8,9},{9,10},{10,1... | collective-permute-start | bytes 98312 | tf_op jit(solution)/shard_map/ppermute | solution.py:20
  187.5 12.6 %collective-permute-start.6 = (bf16[16,1,2,2,4,64]{5,0,4,3,2,1:T(8,128)(2,1)S(1)}, bf16[16,1,2,2,4,64]{5,0,4,3,2,1:T(8,128)(2,1)S(1)}, u32[]{:S(2)}, u32[]{:S(2)}) collective-permute-start(bf16[16,1,2,2,4,64]{5,0,4,3,2,1:T(8,128)(2,1)S(1)} %bitcast.223), channel_id=1, source_target_pairs={{1,0},{2,1},{3,2},{4,3},{5,4},{6,5},{7,6},{8,7},{9,8},{10,9},{11,1... | collective-permute-start | bytes 98312 | tf_op jit(solution)/shard_map/ppermute | solution.py:22
Sparse Core Ops, SparseCore 0:
  11.3 125.8 all-gather.1
where the time goes:
time: 213 us; the launch traced here: 212 us
  waiting for transfers between devices  67.5 us (32%)
  matrix products  41 us (19%)
  starting transfers between devices  37.9 us (18%)
  blocking collectives  36.8 us (17%)
  between operations  16.4 us (8%)
  local copies, waits for them, and re-layouts  10.1 us (5%)
    all_gather x1, waiting for transfers between devices, on_device(): blocks = lax.all_gather(coarse_links, 'group', axis=1, tiled=True)  66.8 us
    all_gather x1, blocking collectives, on_device(): pieces = lax.all_gather(restricted[None], 'group', axis=0, tiled=True)  36.8 us
    dot_general x36, matrix products, hopping(): jnp.einsum('xtyzij,xtyzrj->xtyzri', blocks[direction], shifted[direction]...  34.1 us
    ppermute x4, starting transfers between devices, padded_2(): lax.ppermute(head, axis, [((i + 1) % count, i) for i in range(count)])  27.5 us
    ppermute x4, starting transfers between devices, padded_2(): lax.ppermute(tail, axis, [(i, (i + 1) % count) for i in range(count)])  10.4 us
  transfers between devices with their start and end apart: 9, of which 1 were waited for; matrix products, arithmetic and copies ran while one was open for 19% of the time, Pallas kernels for 0%

commit v1 on v0

v1 whole, which is shorter than its diff:
```python
import functools

import jax
import jax.numpy as jnp
from jax import lax
from jax.experimental import pallas as pl
from jax.experimental.pallas import tpu as pltpu
from jax.sharding import PartitionSpec as P

SPIN_COLOR = 12
NULLV = 32
AGG = 256
COARSE_STEPS = 4
RHS = 4
CDOF = 64
NAGG = 4
FS = NAGG * AGG
FBLOCK = 4
NBLOCK = SPIN_COLOR // FBLOCK
MESH = pl.DeviceIdType.MESH
F32 = jnp.float32
BF16 = jnp.bfloat16


def site_masks(agg_row):
    high = agg_row // 128
    low = agg_row % 128
    lanes = lax.broadcasted_iota(jnp.int32, (128, FS), 0)
    low_hot = jnp.where(lanes == low, 1.0, 0.0).astype(BF16)
    row = lax.broadcasted_iota(jnp.int32, (32, FS), 0)
    place = lax.broadcasted_iota(jnp.int32, (32, FS), 1)
    high_hot = jnp.where((row % 8 == high) & (row // 8 == place // AGG), 1.0, 0.0).astype(BF16)
    grid = lax.dot_general(
        high_hot, low_hot, (((1,), (1,)), ((), ())), preferred_element_type=F32
    )
    return [
        jnp.concatenate([grid[a * 8 + h : a * 8 + h + 1] for h in range(8)], axis=1)
        for a in range(NAGG)
    ]


def fold_lanes(tile):
    tile = tile + pltpu.roll(tile, 64, 1)
    return tile + pltpu.roll(tile, 32, 1)


def restricted_piece(total, row, lane):
    per_agg = []
    for a in range(NAGG):
        parts = []
        for ri in range(2):
            kept = jnp.zeros((8, 128), F32)
            for f in range(FBLOCK):
                at = (f * NAGG + a) * 8
                tile = total[at : at + 8, ri * 128 : (ri + 1) * 128]
                kept = kept + jnp.where(lane // NULLV == f, tile, 0.0)
            parts.append(fold_lanes(kept))
        by_re, by_im = parts
        real = by_re + pltpu.roll(by_im, 4, 0)
        imag = pltpu.roll(by_re, 4, 0) - by_im
        per_agg.append(jnp.where((lane // NULLV) % 2 == 0, real, imag))
    upper = jnp.where(lane < CDOF, per_agg[0], per_agg[1])
    lower = jnp.where(lane < CDOF, per_agg[2], per_agg[3])
    return jnp.where(row < 4, upper, pltpu.roll(lower, 4, 0))


def prolongation_rows(piece, row, lane):
    block = lane // NULLV
    swapped = pltpu.roll(piece, 4, 0)
    doubled = (jnp.where(row < 4, piece, swapped), jnp.where(row < 4, swapped, piece))
    rows = []
    for y in range(2):
        for z in range(2):
            re, im = (
                fold_lanes(jnp.where(block == 2 * z + part, doubled[y], 0.0)) for part in range(2)
            )
            for left, right in ((re, -im), (im, re)):
                for pair in range(2):
                    same = block == 2 * pair + row // RHS
                    rows.append(
                        jnp.concatenate(
                            [jnp.where(same, left, 0.0), jnp.where(same, right, 0.0)], axis=1
                        )
                    )
    return jnp.concatenate(rows, axis=0).astype(BF16)


def build_operator(links, weights):
    zero = jnp.zeros((CDOF, CDOF), BF16)

    def sited(block, z):
        return jnp.concatenate([block, zero] if z == 0 else [zero, block], axis=1)

    for y in range(2):
        for z in range(2):
            n = 2 * y + z
            here = links[0 * 4 + n]
            across = links[(7 + z) * 4 + n]
            columns = [
                jnp.concatenate([here, across] if z == 0 else [across, here], axis=1),
                sited(links[(5 + y) * 4 + n], z),
            ] + [sited(links[k * 4 + n], z) for k in (1, 2, 3, 4)]
            for source, column in enumerate(columns):
                weights[source * 128 : (source + 1) * 128, n * CDOF : (n + 1) * CDOF] = column.T


def hop(weights, here, others, row):
    low = [here, pltpu.roll(here, 4, 0)] + list(others)
    low = jnp.concatenate(low, axis=1).astype(BF16)
    out = jnp.dot(low, weights[...], preferred_element_type=F32)
    return jnp.where(row < 4, out[:, :128], out[:, 128:])


def kernel(
    n_group,
    n_sub,
    owner_ref,
    fine_ref,
    null_ref,
    agg_ref,
    links_ref,
    sol_ref,
    corr_ref,
    fine,
    null,
    agg,
    links,
    weights,
    rhs_out,
    rhs_in,
    iter_out,
    iter_in,
    last_out,
    last_in,
    local_sem,
    rhs_send,
    rhs_recv,
    iter_send,
    iter_recv,
    last_send,
    last_recv,
):
    g = lax.axis_index("group")
    s = lax.axis_index("sub")

    def device(dg, ds):
        return lax.rem(g + dg, n_group), lax.rem(s + ds, n_sub)

    load_agg = pltpu.make_async_copy(agg_ref, agg, local_sem.at[0])
    load_fine = pltpu.make_async_copy(fine_ref, fine, local_sem.at[1])
    load_links = pltpu.make_async_copy(links_ref, links, local_sem.at[2])
    load_null = [
        pltpu.make_async_copy(
            null_ref.at[:, pl.ds(b * FBLOCK, FBLOCK)],
            null.at[:, pl.ds(b * FBLOCK, FBLOCK)],
            local_sem.at[3 + b],
        )
        for b in range(NBLOCK)
    ]
    load_agg.start()
    load_fine.start()
    for load in load_null:
        load.start()
    load_links.start()

    barrier = pltpu.get_barrier_semaphore()
    n_far = 3 * n_group - 1

    def offsets(i):
        at = i // n_group
        return lax.rem(i, n_group), lax.rem(at * (n_sub - 1) + (at // 2) * 3, n_sub)

    def greet(i, carry):
        pl.semaphore_signal(barrier, inc=1, device_id=device(*offsets(i)), device_id_type=MESH)
        return carry

    lax.fori_loop(1, n_far + 1, greet, 0)

    row = lax.broadcasted_iota(jnp.int32, (8, 128), 0)
    lane = lax.broadcasted_iota(jnp.int32, (8, 128), 1)

    load_agg.wait()
    masks = site_masks(agg[...])
    load_fine.wait()
    total = jnp.zeros((128, 256), F32)
    for b in range(NBLOCK):
        spread = []
        for f in range(b * FBLOCK, (b + 1) * FBLOCK):
            psi = jnp.concatenate([fine[0, f].astype(F32), fine[1, f].astype(F32)], axis=0)
            spread += [psi * masks[a] for a in range(NAGG)]
        spread = jnp.concatenate(spread, axis=0).astype(BF16)
        load_null[b].wait()
        part = null[:, b * FBLOCK : (b + 1) * FBLOCK].reshape(2 * FBLOCK * NULLV, FS)
        total = total + lax.dot_general(
            spread, part, (((1,), (1,)), ((), ())), preferred_element_type=F32
        )
    mine = restricted_piece(total, row, lane).astype(BF16)
    rhs_out[...] = mine
    rhs_in[0, g] = mine

    pl.semaphore_wait(barrier, n_far)

    def rhs_copy(i):
        dg, ds = offsets(i)
        at = i // n_group
        return pltpu.make_async_remote_copy(
            src_ref=rhs_out,
            dst_ref=rhs_in.at[at, g],
            send_sem=rhs_send.at[i],
            recv_sem=rhs_recv.at[at, g],
            device_id=device(dg, ds),
            device_id_type=MESH,
        )

    def rhs_start(i, carry):
        rhs_copy(i).start()
        return carry

    lax.fori_loop(1, n_far + 1, rhs_start, 0)

    load_links.wait()
    build_operator(links, weights)

    def rhs_wait(i, carry):
        at = i // n_group
        source = lax.rem(g + i, n_group)
        pltpu.make_async_remote_copy(
            src_ref=rhs_out,
            dst_ref=rhs_in.at[at, source],
            send_sem=rhs_send.at[i],
            recv_sem=rhs_recv.at[at, source],
            device_id=device(0, 1),
            device_id_type=MESH,
        ).wait_recv()
        return carry

    lax.fori_loop(1, n_far + 1, rhs_wait, 0)

    def chosen(at, x):
        picked = jnp.zeros((8, 128), F32)
        for k in range(n_group):
            picked = picked + jnp.where(owner_ref[k] == x, rhs_in[at, k].astype(F32), 0.0)
        return picked

    ahead_x = lax.rem(g + 1, n_group)
    behind_x = lax.rem(g + n_group - 1, n_group)
    rhs = chosen(0, g)
    others = [chosen(0, ahead_x), chosen(0, behind_x), chosen(1, g), chosen(2, g)]
    iterate = rhs - hop(weights, rhs, others, row)

    steps = [(n_group - 1, 0), (1, 0), (0, n_sub - 1), (0, 1)]
    pending = []
    for step in range(COARSE_STEPS - 1):
        iter_out[step] = iterate
        copies = [
            pltpu.make_async_remote_copy(
                src_ref=iter_out.at[step],
                dst_ref=iter_in.at[step, way],
                send_sem=iter_send.at[step, way],
                recv_sem=iter_recv.at[step, way],
                device_id=device(*steps[way]),
                device_id_type=MESH,
            )
            for way in range(4)
        ]
        for copy in copies:
            copy.start()
        for copy in copies:
            copy.wait_recv()
        pending += copies
        iterate = rhs - hop(weights, iterate, [iter_in[step, way] for way in range(4)], row)

    rounded = iterate.astype(BF16)
    last_out[...] = rounded
    last_in[g] = rounded

    def last_copy(i, at):
        return pltpu.make_async_remote_copy(
            src_ref=last_out,
            dst_ref=last_in.at[at],
            send_sem=last_send.at[i],
            recv_sem=last_recv.at[at],
            device_id=device(i, 0),
            device_id_type=MESH,
        )

    def last_start(i, carry):
        last_copy(i, g).start()
        return carry

    lax.fori_loop(1, n_group, last_start, 0)
    for y in range(2):
        for z in range(2):
            sol_ref[y, z] = iterate[y * RHS : (y + 1) * RHS, z * CDOF : (z + 1) * CDOF]

    def last_wait(i, carry):
        last_copy(i, lax.rem(g + i, n_group)).wait_recv()
        return carry

    lax.fori_loop(1, n_group, last_wait, 0)

    block_here = jnp.int32(0)
    for k in range(n_group):
        block_here = block_here + jnp.where(g == k, owner_ref[k], 0)
    own = jnp.zeros((8, 128), F32)
    for k in range(n_group):
        own = own + jnp.where(block_here == k, last_in[k].astype(F32), 0.0)

    left = prolongation_rows(own, row, lane)
    for b in range(NBLOCK):
        part = null[:, b * FBLOCK : (b + 1) * FBLOCK].reshape(2 * FBLOCK * NULLV, FS)
        wide = jnp.dot(left, part, preferred_element_type=F32)
        here = wide[:32] * masks[0]
        for a in range(1, NAGG):
            here = here + wide[a * 32 : (a + 1) * 32] * masks[a]
        for ri in range(2):
            for f in range(FBLOCK):
                at = (ri * FBLOCK + f) * RHS
                corr_ref[ri, b * FBLOCK + f] = here[at : at + RHS].astype(BF16)

    def rhs_done(i, carry):
        rhs_copy(i).wait_send()
        return carry

    lax.fori_loop(1, n_far + 1, rhs_done, 0)
    for copy in pending:
        copy.wait_send()

    def last_done(i, carry):
        last_copy(i, g).wait_send()
        return carry

    lax.fori_loop(1, n_group, last_done, 0)


def on_device(n_group, n_sub, fine_residual, null_vectors, agg_map, block_owner, coarse_links):
    any_space = pl.BlockSpec(memory_space=pl.ANY)
    vmem = pl.BlockSpec(memory_space=pltpu.VMEM)
    dma = pltpu.SemaphoreType.DMA
    exchanges = COARSE_STEPS - 1
    solution_here, correction = pl.pallas_call(
        functools.partial(kernel, n_group, n_sub),
        out_shape=(
            jax.ShapeDtypeStruct((2, 2, RHS, CDOF), F32),
            jax.ShapeDtypeStruct((2, SPIN_COLOR, RHS, FS), BF16),
        ),
        in_specs=[pl.BlockSpec(memory_space=pltpu.SMEM)] + [any_space] * 4,
        out_specs=(vmem, vmem),
        scratch_shapes=[
            pltpu.VMEM((2, SPIN_COLOR, RHS, FS), BF16),
            pltpu.VMEM((2, SPIN_COLOR, NULLV, FS), BF16),
            pltpu.VMEM((1, FS), jnp.int32),
            pltpu.VMEM((36, CDOF, CDOF), BF16),
            pltpu.VMEM((6 * 128, 256), BF16),
            pltpu.VMEM((8, 128), BF16),
            pltpu.VMEM((3, n_group, 8, 128), BF16),
            pltpu.VMEM((exchanges, 8, 128), F32),
            pltpu.VMEM((exchanges, 4, 8, 128), F32),
            pltpu.VMEM((8, 128), BF16),
            pltpu.VMEM((n_group, 8, 128), BF16),
            dma((3 + NBLOCK,)),
            dma((3 * n_group,)),
            dma((3, n_group)),
            dma((exchanges, 4)),
            dma((exchanges, 4)),
            dma((n_group,)),
            dma((n_group,)),
        ],
        compiler_params=pltpu.CompilerParams(
            collective_id=0, has_side_effects=True, vmem_limit_bytes=32 * 1024 * 1024
        ),
    )(
        block_owner,
        fine_residual,
        null_vectors,
        agg_map,
        coarse_links.reshape(36, CDOF, CDOF),
    )
    return solution_here.reshape(1, 1, 2, 2, RHS, CDOF), correction


def solution(mesh):
    in_specs = (
        P(None, None, None, ("group", "sub")),
        P(None, None, None, ("group", "sub")),
        P(("group", "sub"), None),
        P(),
        P(None, "group", "sub", None, None, None, None),
    )
    out_specs = (P("group", "sub", None, None, None, None), P(None, None, None, ("group", "sub")))
    return jax.shard_map(
        functools.partial(on_device, mesh.shape["group"], mesh.shape["sub"]),
        mesh=mesh,
        in_specs=in_specs,
        out_specs=out_specs,
        check_vma=False,
    )
```

time: 213 us -> 56.8 us (0.27)
  waiting for transfers between devices: 67.5 us -> 0 us
  Pallas kernels: 0 us -> 49.9 us
  matrix products: 41 us -> 0 us
  starting transfers between devices: 37.9 us -> 0 us
  blocking collectives: 36.8 us -> 0 us
  between operations: 16.4 us -> 0.65 us
  local copies, waits for them, and re-layouts: 10.1 us -> 6.01 us
    all_gather x1 -> x0, waiting for transfers between devices: 66.8 us -> none  [on_device(): blocks = lax.all_gather(coarse_links, 'group', axis=1, tiled=True)]
    pallas_call x0 -> x1, Pallas kernels: none -> 49.9 us  [on_device(): pl.pallas_call(functools.partial(kernel, n_group, n_sub), out_shape=(jax....]
    dot_general x48 -> x0, matrix products: 41 us -> none  [the longest x36 34.1 us: hopping(): jnp.einsum('xtyzij,xtyzrj->xtyzri', blocks[direction], shifted[direction]...]
    ppermute x8 -> x0, starting transfers between devices: 37.9 us -> none  [the longest x4 27.5 us: padded_2(): lax.ppermute(head, axis, [((i + 1) % count, i) for i in range(count)])]
    all_gather x1 -> x0, blocking collectives: 36.8 us -> none  [on_device(): pieces = lax.all_gather(restricted[None], 'group', axis=0, tiled=True)]
    unnamed x12, local copies, waits for them, and re-layouts: 0.72 us -> 6.01 us
    slice x12 -> x0, local copies, waits for them, and re-layouts: 3.81 us -> none  [the longest x2 3.35 us: on_device(): null_agg[1]]
    squeeze x4 -> x0, local copies, waits for them, and re-layouts: 2.61 us -> none  [the longest x1 1.95 us: on_device(): null_agg[1]]
  transfers between devices with their start and end apart: 9 -> 0, of which waited for: 1 -> 0; matrix products, arithmetic and copies ran while one was open for 19% -> 0% of each run, Pallas kernels for 0% -> 0%
where the time goes in v1:
time: 56.8 us; the launch traced here: 56.5 us
  Pallas kernels  49.9 us (88%)
  local copies, waits for them, and re-layouts  6.01 us (11%)
  between operations  0.65 us (1%)
    pallas_call x1, Pallas kernels, on_device(): pl.pallas_call(functools.partial(kernel, n_group, n_sub), out_shape=(jax....  49.9 us
    unnamed x12, local copies, waits for them, and re-layouts  6.01 us

profile of v1, /device:TPU:1, one launch (start us, length us, event | category | flops | bytes accessed | tf_op | source)
XLA Modules:
  0.0 56.5 jit_solution(2662544225756588356)
XLA Ops:
  0.6 0.0 copy-start
  0.6 1.4 %copy-done = bf16[2,12,32,1024]{3,2,1,0:T(8,128)(2,1)S(1)} copy-done((bf16[2,12,32,1024]{3,2,1,0:T(8,128)(2,1)S(1)}, bf16[2,12,32,1024]{3,2,1,0:T(8,128)(2,1)}, u32[]{:S(2)}) %copy-start) | copy-done | bytes 1572888
  2.0 0.0 copy-start.1
  2.0 1.1 %copy-done.1 = bf16[9,1,1,2,2,64,64]{6,5,4,3,2,1,0:T(8,128)(2,1)S(1)} copy-done((bf16[9,1,1,2,2,64,64]{6,5,4,3,2,1,0:T(8,128)(2,1)S(1)}, bf16[9,1,1,2,2,64,64]{6,5,4,3,2,1,0:T(8,128)(2,1)}, u32[]{:S(2)}) %copy-start.1) | copy-done | bytes 294936
  3.1 0.0 copy-start.2
  3.1 0.9 %copy-done.2 = bf16[2,12,4,1024]{3,2,1,0:T(4,128)(2,1)S(1)} copy-done((bf16[2,12,4,1024]{3,2,1,0:T(4,128)(2,1)S(1)}, bf16[2,12,4,1024]{3,2,1,0:T(4,128)(2,1)}, u32[]{:S(2)}) %copy-start.2) | copy-done | bytes 196632
  4.0 0.0 copy-start.3
  4.0 0.7 %copy-done.3 = s32[1,1024]{1,0:T(1,128)S(1)} copy-done((s32[1,1024]{1,0:T(1,128)S(1)}, s32[1,1024]{1,0:T(1,128)}, u32[]{:S(2)}) %copy-start.3) | copy-done | bytes 4120
  4.7 0.0 copy-start.4
  4.7 0.7 %copy-done.4 = s32[16]{0:T(128)S(1)} copy-done((s32[16]{0:T(128)S(1)}, s32[16]{0:T(128)}, u32[]{:S(2)}) %copy-start.4) | copy-done | bytes 88
  5.4 49.9 %shard_map.68 = (f32[2,2,4,64]{3,2,1,0:T(4,128)S(1)}, bf16[2,12,4,1024]{3,2,1,0:T(4,128)(2,1)S(1)}) custom-call(s32[16]{0:T(128)S(1)} %copy-done.4, bf16[2,12,4,1024]{3,2,1,0:T(4,128)(2,1)S(1)} %copy-done.2, bf16[2,12,32,1024]{3,2,1,0:T(8,128)(2,1)S(1)} %copy-done, s32[1,1024]{1,0:T(1,128)S(1)} %copy-done.3, bf16[36,64,64]{2,1,0:T(8,128)(2,1)S(1)} %bitcast.2), custom_call_target="tpu_custom_call" | custom-call | tf_op jit(solution)/shard_map/pallas_call | solution.py:341
  55.2 0.6 %copy.9 = f32[1,1,2,2,4,64]{5,4,3,2,1,0:T(4,128)} copy(f32[1,1,2,2,4,64]{5,4,3,2,1,0:T(4,128)S(1)} %bitcast.3) | data formatting | bytes 8192
  55.8 0.7 %copy.10 = bf16[2,12,4,1024]{3,2,1,0:T(4,128)(2,1)} copy(bf16[2,12,4,1024]{3,2,1,0:T(4,128)(2,1)S(1)} %get-tuple-element.9) | data formatting | bytes 393216
Async XLA Ops:
  0.6 1.4 %copy-start = (bf16[2,12,32,1024]{3,2,1,0:T(8,128)(2,1)S(1)}, bf16[2,12,32,1024]{3,2,1,0:T(8,128)(2,1)}, u32[]{:S(2)}) copy-start(bf16[2,12,32,1024]{3,2,1,0:T(8,128)(2,1)} %null_ref.1) | copy-start | bytes 4718596
  2.0 1.1 %copy-start.1 = (bf16[9,1,1,2,2,64,64]{6,5,4,3,2,1,0:T(8,128)(2,1)S(1)}, bf16[9,1,1,2,2,64,64]{6,5,4,3,2,1,0:T(8,128)(2,1)}, u32[]{:S(2)}) copy-start(bf16[9,1,1,2,2,64,64]{6,5,4,3,2,1,0:T(8,128)(2,1)} %param.9) | copy-start | bytes 884740
  3.1 0.9 %copy-start.2 = (bf16[2,12,4,1024]{3,2,1,0:T(4,128)(2,1)S(1)}, bf16[2,12,4,1024]{3,2,1,0:T(4,128)(2,1)}, u32[]{:S(2)}) copy-start(bf16[2,12,4,1024]{3,2,1,0:T(4,128)(2,1)} %fine_ref.1) | copy-start | bytes 589828
  4.0 0.7 %copy-start.3 = (s32[1,1024]{1,0:T(1,128)S(1)}, s32[1,1024]{1,0:T(1,128)}, u32[]{:S(2)}) copy-start(s32[1,1024]{1,0:T(1,128)} %agg_ref.1) | copy-start | bytes 12292
  4.7 0.7 %copy-start.4 = (s32[16]{0:T(128)S(1)}, s32[16]{0:T(128)}, u32[]{:S(2)}) copy-start(s32[16]{0:T(128)} %owner_ref.1) | copy-start | bytes 196

commit v2 on v1

--- a/solution.py
+++ b/solution.py
@@ -62,6 +62,23 @@
     upper = jnp.where(lane < CDOF, per_agg[0], per_agg[1])
     lower = jnp.where(lane < CDOF, per_agg[2], per_agg[3])
     return jnp.where(row < 4, upper, pltpu.roll(lower, 4, 0))
+
+
+def restrict(fine, null, masks, row, lane, loads=()):
+    total = jnp.zeros((128, 256), F32)
+    for b in range(NBLOCK):
+        spread = []
+        for f in range(b * FBLOCK, (b + 1) * FBLOCK):
+            psi = jnp.concatenate([fine[0, f].astype(F32), fine[1, f].astype(F32)], axis=0)
+            spread += [psi * masks[a] for a in range(NAGG)]
+        spread = jnp.concatenate(spread, axis=0).astype(BF16)
+        for load in loads[b : b + 1]:
+            load.wait()
+        part = null[:, b * FBLOCK : (b + 1) * FBLOCK].reshape(2 * FBLOCK * NULLV, FS)
+        total = total + lax.dot_general(
+            spread, part, (((1,), (1,)), ((), ())), preferred_element_type=F32
+        )
+    return restricted_piece(total, row, lane)
 
 
 def prolongation_rows(piece, row, lane):
@@ -85,6 +102,34 @@
     return jnp.concatenate(rows, axis=0).astype(BF16)
 
 
+def prolong_kernel(sol_ref, own_ref, masks_ref, null, sol_out, corr_out, sol, corr, sem):
+    row = lax.broadcasted_iota(jnp.int32, (8, 128), 0)
+    lane = lax.broadcasted_iota(jnp.int32, (8, 128), 1)
+    for y in range(2):
+        for z in range(2):
+            sol[y, z] = sol_ref[y * RHS : (y + 1) * RHS, z * CDOF : (z + 1) * CDOF]
+    stores = [pltpu.make_async_copy(sol, sol_out, sem.at[NBLOCK])]
+    stores[0].start()
+    left = prolongation_rows(own_ref[...], row, lane)
+    for b in range(NBLOCK):
+        at_f = pl.ds(b * FBLOCK, FBLOCK)
+        part = null[:, b * FBLOCK : (b + 1) * FBLOCK].reshape(2 * FBLOCK * NULLV, FS)
+        wide = jnp.dot(left, part, preferred_element_type=F32)
+        here = wide[:32] * masks_ref[0:1]
+        for a in range(1, NAGG):
+            here = here + wide[a * 32 : (a + 1) * 32] * masks_ref[a : a + 1]
+        for ri in range(2):
+            for f in range(FBLOCK):
+                at = (ri * FBLOCK + f) * RHS
+                corr[ri, b * FBLOCK + f] = here[at : at + RHS].astype(BF16)
+        stores.append(
+            pltpu.make_async_copy(corr.at[:, at_f], corr_out.at[:, at_f], sem.at[b])
+        )
+        stores[-1].start()
+    for store in stores:
+        store.wait()
+
+
 def build_operator(links, weights):
     zero = jnp.zeros((CDOF, CDOF), BF16)
 
@@ -120,11 +165,13 @@
     agg_ref,
     links_ref,
     sol_ref,
-    corr_ref,
+    own_ref,
+    masks_ref,
+    null,
     fine,
-    null,
     agg,
     links,
+    owner,
     weights,
     rhs_out,
     rhs_in,
@@ -157,11 +204,13 @@
         )
         for b in range(NBLOCK)
     ]
+    load_owner = pltpu.make_async_copy(owner_ref, owner, local_sem.at[3 + NBLOCK])
     load_agg.start()
     load_fine.start()
     for load in load_null:
         load.start()
     load_links.start()
+    load_owner.start()
 
     barrier = pltpu.get_barrier_semaphore()
     n_far = 3 * n_group - 1
@@ -181,20 +230,10 @@
 
     load_agg.wait()
     masks = site_masks(agg[...])
+    for a in range(NAGG):
+        masks_ref[a : a + 1] = masks[a]
     load_fine.wait()
-    total = jnp.zeros((128, 256), F32)
-    for b in range(NBLOCK):
-        spread = []
-        for f in range(b * FBLOCK, (b + 1) * FBLOCK):
-            psi = jnp.concatenate([fine[0, f].astype(F32), fine[1, f].astype(F32)], axis=0)
-            spread += [psi * masks[a] for a in range(NAGG)]
-        spread = jnp.concatenate(spread, axis=0).astype(BF16)
-        load_null[b].wait()
-        part = null[:, b * FBLOCK : (b + 1) * FBLOCK].reshape(2 * FBLOCK * NULLV, FS)
-        total = total + lax.dot_general(
-            spread, part, (((1,), (1,)), ((), ())), preferred_element_type=F32
-        )
-    mine = restricted_piece(total, row, lane).astype(BF16)
+    mine = restrict(fine, null, masks, row, lane, load_null).astype(BF16)
     rhs_out[...] = mine
     rhs_in[0, g] = mine
 
@@ -219,6 +258,7 @@
     lax.fori_loop(1, n_far + 1, rhs_start, 0)
 
     load_links.wait()
+    load_owner.wait()
     build_operator(links, weights)
 
     def rhs_wait(i, carry):
@@ -239,7 +279,7 @@
     def chosen(at, x):
         picked = jnp.zeros((8, 128), F32)
         for k in range(n_group):
-            picked = picked + jnp.where(owner_ref[k] == x, rhs_in[at, k].astype(F32), 0.0)
+            picked = picked + jnp.where(owner[k] == x, rhs_in[at, k].astype(F32), 0.0)
         return picked
 
     ahead_x = lax.rem(g + 1, n_group)
@@ -289,9 +329,7 @@
         return carry
 
     lax.fori_loop(1, n_group, last_start, 0)
-    for y in range(2):
-        for z in range(2):
-            sol_ref[y, z] = iterate[y * RHS : (y + 1) * RHS, z * CDOF : (z + 1) * CDOF]
+    sol_ref[...] = iterate
 
     def last_wait(i, carry):
         last_copy(i, lax.rem(g + i, n_group)).wait_recv()
@@ -301,22 +339,12 @@
 
     block_here = jnp.int32(0)
     for k in range(n_group):
-        block_here = block_here + jnp.where(g == k, owner_ref[k], 0)
+        block_here = block_here + jnp.where(g == k, owner[k], 0)
     own = jnp.zeros((8, 128), F32)
     for k in range(n_group):
         own = own + jnp.where(block_here == k, last_in[k].astype(F32), 0.0)
 
-    left = prolongation_rows(own, row, lane)
-    for b in range(NBLOCK):
-        part = null[:, b * FBLOCK : (b + 1) * FBLOCK].reshape(2 * FBLOCK * NULLV, FS)
-        wide = jnp.dot(left, part, preferred_element_type=F32)
-        here = wide[:32] * masks[0]
-        for a in range(1, NAGG):
-            here = here + wide[a * 32 : (a + 1) * 32] * masks[a]
-        for ri in range(2):
-            for f in range(FBLOCK):
-                at = (ri * FBLOCK + f) * RHS
-                corr_ref[ri, b * FBLOCK + f] = here[at : at + RHS].astype(BF16)
+    own_ref[...] = own
 
     def rhs_done(i, carry):
         rhs_copy(i).wait_send()
@@ -334,23 +362,26 @@
 
 
 def on_device(n_group, n_sub, fine_residual, null_vectors, agg_map, block_owner, coarse_links):
-    any_space = pl.BlockSpec(memory_space=pl.ANY)
+    hbm = pl.BlockSpec(memory_space=pltpu.HBM)
     vmem = pl.BlockSpec(memory_space=pltpu.VMEM)
     dma = pltpu.SemaphoreType.DMA
     exchanges = COARSE_STEPS - 1
-    solution_here, correction = pl.pallas_call(
+    in_hbm = functools.partial(pltpu.with_memory_space_constraint, memory_space=pltpu.HBM)
+    solved = pl.pallas_call(
         functools.partial(kernel, n_group, n_sub),
         out_shape=(
-            jax.ShapeDtypeStruct((2, 2, RHS, CDOF), F32),
-            jax.ShapeDtypeStruct((2, SPIN_COLOR, RHS, FS), BF16),
+            jax.ShapeDtypeStruct((8, 128), F32),
+            jax.ShapeDtypeStruct((8, 128), F32),
+            jax.ShapeDtypeStruct((NAGG, FS), F32),
+            jax.ShapeDtypeStruct((2, SPIN_COLOR, NULLV, FS), BF16),
         ),
-        in_specs=[pl.BlockSpec(memory_space=pltpu.SMEM)] + [any_space] * 4,
-        out_specs=(vmem, vmem),
+        in_specs=[hbm] * 5,
+        out_specs=(vmem,) * 4,
         scratch_shapes=[
             pltpu.VMEM((2, SPIN_COLOR, RHS, FS), BF16),
-            pltpu.VMEM((2, SPIN_COLOR, NULLV, FS), BF16),
             pltpu.VMEM((1, FS), jnp.int32),
             pltpu.VMEM((36, CDOF, CDOF), BF16),
+            pltpu.SMEM((n_group,), jnp.int32),
             pltpu.VMEM((6 * 128, 256), BF16),
             pltpu.VMEM((8, 128), BF16),
             pltpu.VMEM((3, n_group, 8, 128), BF16),
@@ -358,7 +389,7 @@
             pltpu.VMEM((exchanges, 4, 8, 128), F32),
             pltpu.VMEM((8, 128), BF16),
             pltpu.VMEM((n_group, 8, 128), BF16),
-            dma((3 + NBLOCK,)),
+            dma((4 + NBLOCK,)),
             dma((3 * n_group,)),
             dma((3, n_group)),
             dma((exchanges, 4)),
@@ -367,15 +398,32 @@
             dma((n_group,)),
         ],
         compiler_params=pltpu.CompilerParams(
-            collective_id=0, has_side_effects=True, vmem_limit_bytes=32 * 1024 * 1024
+            collective_id=0, has_side_effects=True, vmem_limit_bytes=24 * 1024 * 1024
         ),
+        name="coarse",
     )(
-        block_owner,
-        fine_residual,
-        null_vectors,
-        agg_map,
-        coarse_links.reshape(36, CDOF, CDOF),
+        in_hbm(block_owner),
+        in_hbm(fine_residual),
+        in_hbm(null_vectors),
+        in_hbm(agg_map),
+        in_hbm(coarse_links.reshape(36, CDOF, CDOF)),
     )
+    solution_here, correction = pl.pallas_call(
+        prolong_kernel,
+        out_shape=(
+            jax.ShapeDtypeStruct((2, 2, RHS, CDOF), F32),
+            jax.ShapeDtypeStruct((2, SPIN_COLOR, RHS, FS), BF16),
+        ),
+        in_specs=[vmem] * 4,
+        out_specs=(hbm, hbm),
+        scratch_shapes=[
+            pltpu.VMEM((2, 2, RHS, CDOF), F32),
+            pltpu.VMEM((2, SPIN_COLOR, RHS, FS), BF16),
+            dma((1 + NBLOCK,)),
+        ],
+        compiler_params=pltpu.CompilerParams(vmem_limit_bytes=24 * 1024 * 1024),
+        name="prolong",
+    )(*solved)
     return solution_here.reshape(1, 1, 2, 2, RHS, CDOF), correction
 
 

time: 56.8 us -> 50.2 us (0.88)
  local copies, waits for them, and re-layouts: 6.01 us -> 0 us
    unnamed x12 -> x0, local copies, waits for them, and re-layouts: 6.01 us -> none
    pallas_call x1, Pallas kernels: 49.9 us -> 48.2 us  [on_device(): pl.pallas_call(functools.partial(kernel, n_group, n_sub), out_shape=(jax....]
    pallas_call x0 -> x1, Pallas kernels: none -> 1.17 us  [on_device(): pl.pallas_call(prolong_kernel, out_shape=(jax.ShapeDtypeStruct((2, 2, RHS...]
where the time goes in v2:
time: 50.2 us; the launch traced here: 50 us
  Pallas kernels  49.4 us (98%)
  between operations  0.64 us (1%)
    pallas_call x1, Pallas kernels, on_device(): pl.pallas_call(functools.partial(kernel, n_group, n_sub), out_shape=(jax....  48.2 us
    pallas_call x1, Pallas kernels, on_device(): pl.pallas_call(prolong_kernel, out_shape=(jax.ShapeDtypeStruct((2, 2, RHS...  1.17 us

profile of v2, /device:TPU:1, one launch (start us, length us, event | category | flops | bytes accessed | tf_op | source)
XLA Modules:
  0.0 50.0 jit_solution(3589441427816103060)
XLA Ops:
  0.6 48.2 %coarse.1 = (f32[8,128]{1,0:T(8,128)S(1)}, f32[8,128]{1,0:T(8,128)S(1)}, f32[4,1024]{1,0:T(4,128)S(1)}, bf16[2,12,32,1024]{3,2,1,0:T(8,128)(2,1)S(1)}) custom-call(s32[16]{0:T(128)} %owner_ref.1, bf16[2,12,4,1024]{3,2,1,0:T(4,128)(2,1)} %fine_ref.1, bf16[2,12,32,1024]{3,2,1,0:T(8,128)(2,1)} %null_ref.1, s32[1,1024]{1,0:T(1,128)} %agg_ref.1, ...), custom_call_target="tpu_custom_call" | custom-call | tf_op jit(solution)/shard_map/coarse/pallas_call | solution.py:370
  48.9 1.2 %prolong.1 = (f32[2,2,4,64]{3,2,1,0:T(4,128)}, bf16[2,12,4,1024]{3,2,1,0:T(4,128)(2,1)}) custom-call(f32[8,128]{1,0:T(8,128)S(1)} %get-tuple-element.8.sol_ref, f32[8,128]{1,0:T(8,128)S(1)} %get-tuple-element.9.own_ref, f32[4,1024]{1,0:T(4,128)S(1)} %get-tuple-element.10.masks_ref, bf16[2,12,32,1024]{3,2,1,0:T(8,128)(2,1)S(1)} %get-tuple-element.11.null), custom_call_target="tpu_custom_call" | custom-call | tf_op jit(solution)/shard_map/prolong/pallas_call | solution.py:411

commit v3 on v2

--- a/solution.py
+++ b/solution.py
@@ -152,8 +152,20 @@
 def hop(weights, here, others, row):
     low = [here, pltpu.roll(here, 4, 0)] + list(others)
     low = jnp.concatenate(low, axis=1).astype(BF16)
-    out = jnp.dot(low, weights[...], preferred_element_type=F32)
+    out = jnp.dot(low, weights[: len(others) * 128 + 256], preferred_element_type=F32)
     return jnp.where(row < 4, out[:, :128], out[:, 128:])
+
+
+def pushes(toward, here, row, lane):
+    low = jnp.concatenate([jnp.where(lane < CDOF, here, 0.0), jnp.where(lane < CDOF, 0.0, here)], axis=0)
+    out = jnp.dot(low.astype(BF16), toward[...], preferred_element_type=F32)
+    parts = []
+    for k in range(4):
+        low_z, high_z = out[:8, k * 128 : (k + 1) * 128], out[8:, k * 128 : (k + 1) * 128]
+        low_z = jnp.where(row < 4, low_z, pltpu.roll(low_z, CDOF, 1))
+        high_z = jnp.where(row < 4, pltpu.roll(high_z, CDOF, 1), high_z)
+        parts.append(jnp.where(lane < CDOF, low_z, high_z))
+    return parts
 
 
 def kernel(
@@ -173,25 +185,55 @@
     links,
     owner,
     weights,
+    toward,
+    link_out,
+    link_in,
     rhs_out,
     rhs_in,
-    iter_out,
-    iter_in,
+    near_out,
+    near_in,
+    far_out,
+    far_in,
+    skew_out,
+    skew_in,
     last_out,
     last_in,
+    turn_out,
+    turn_in,
     local_sem,
+    link_send,
+    link_recv,
     rhs_send,
     rhs_recv,
-    iter_send,
-    iter_recv,
+    mid_send,
+    mid_recv,
     last_send,
     last_recv,
 ):
     g = lax.axis_index("group")
     s = lax.axis_index("sub")
+    half = n_group // 2
+    chips = n_group // 4
+    at_x, at_y, at_core = g // 4, (g // 2) % 2, g % 2
 
     def device(dg, ds):
-        return lax.rem(g + dg, n_group), lax.rem(s + ds, n_sub)
+        return lax.rem(g + (dg + n_group), n_group), lax.rem(s + (ds + n_sub), n_sub)
+
+    def member(flip, i):
+        x = lax.rem(at_x + (chips - 1 - i // 2), chips)
+        return x * 4 + lax.rem(at_y + flip, 2) * 2 + lax.rem(at_core + 1 - i % 2, 2)
+
+    def remote(src, dst, send, recv, to):
+        return pltpu.make_async_remote_copy(
+            src_ref=src, dst_ref=dst, send_sem=send, recv_sem=recv, device_id=to, device_id_type=MESH
+        )
+
+    def each(count, body):
+        def run(i, carry):
+            body(i)
+            return carry
+
+        lax.fori_loop(0, count, run, 0)
 
     load_agg = pltpu.make_async_copy(agg_ref, agg, local_sem.at[0])
     load_fine = pltpu.make_async_copy(fine_ref, fine, local_sem.at[1])
@@ -212,18 +254,18 @@
     load_links.start()
     load_owner.start()
 
+    to_t = (0, -1, 1)
     barrier = pltpu.get_barrier_semaphore()
-    n_far = 3 * n_group - 1
-
-    def offsets(i):
-        at = i // n_group
-        return lax.rem(i, n_group), lax.rem(at * (n_sub - 1) + (at // 2) * 3, n_sub)
-
-    def greet(i, carry):
-        pl.semaphore_signal(barrier, inc=1, device_id=device(*offsets(i)), device_id_type=MESH)
-        return carry
-
-    lax.fori_loop(1, n_far + 1, greet, 0)
+
+    def greet(to):
+        pl.semaphore_signal(barrier, inc=1, device_id=to, device_id_type=MESH)
+
+    for at in (2, 1, 0):
+        for flip in (1, 0):
+            count = half - 1 if at == 0 and flip == 0 else half
+            each(count, lambda i: greet((member(flip, i), device(0, to_t[at])[1])))
+    greet(device(0, 2))
+    greet(device(0, -2))
 
     row = lax.broadcasted_iota(jnp.int32, (8, 128), 0)
     lane = lax.broadcasted_iota(jnp.int32, (8, 128), 1)
@@ -237,44 +279,51 @@
     rhs_out[...] = mine
     rhs_in[0, g] = mine
 
-    pl.semaphore_wait(barrier, n_far)
-
-    def rhs_copy(i):
-        dg, ds = offsets(i)
-        at = i // n_group
-        return pltpu.make_async_remote_copy(
-            src_ref=rhs_out,
-            dst_ref=rhs_in.at[at, g],
-            send_sem=rhs_send.at[i],
-            recv_sem=rhs_recv.at[at, g],
-            device_id=device(dg, ds),
-            device_id_type=MESH,
-        )
-
-    def rhs_start(i, carry):
-        rhs_copy(i).start()
-        return carry
-
-    lax.fori_loop(1, n_far + 1, rhs_start, 0)
-
+    pl.semaphore_wait(barrier, 3 * n_group - 1 + 2)
+
+    def rhs_copy(at, flip, i):
+        return remote(
+            rhs_out,
+            rhs_in.at[at, g],
+            rhs_send.at[at, flip * half + i],
+            rhs_recv.at[at, g],
+            (member(flip, i), device(0, to_t[at])[1]),
+        )
+
+    broadcast = [
+        (at, flip, half - 1 if at == 0 and flip == 0 else half) for flip in (1, 0) for at in (2, 1, 0)
+    ]
+    for at, flip, count in broadcast:
+        each(count, lambda i: rhs_copy(at, flip, i).start())
+
+    ahead = ((1, 0), (-1, 0), (0, 1), (0, -1))
     load_links.wait()
+    link_copies = []
+    for k in range(4):
+        for y in range(2):
+            at = (k + 1) * 4 + 2 * y
+            link_out[k, y * CDOF : (y + 1) * CDOF] = jnp.concatenate(
+                [links[at], links[at + 1]], axis=1
+            )
+        copy = remote(
+            link_out.at[k], link_in.at[k], link_send.at[k], link_recv.at[k], device(*ahead[k])
+        )
+        copy.start()
+        link_copies.append(copy)
+    build_operator(links, weights)
     load_owner.wait()
-    build_operator(links, weights)
-
-    def rhs_wait(i, carry):
-        at = i // n_group
-        source = lax.rem(g + i, n_group)
-        pltpu.make_async_remote_copy(
-            src_ref=rhs_out,
-            dst_ref=rhs_in.at[at, source],
-            send_sem=rhs_send.at[i],
-            recv_sem=rhs_recv.at[at, source],
-            device_id=device(0, 1),
-            device_id_type=MESH,
+    for k, copy in enumerate(link_copies):
+        copy.wait_recv()
+        toward[:, k * 128 : (k + 1) * 128] = link_in[k].T
+
+    def rhs_wait(at, flip, i):
+        source = member(flip, i)
+        remote(
+            rhs_out, rhs_in.at[at, source], rhs_send.at[at, 0], rhs_recv.at[at, source], device(0, 1)
         ).wait_recv()
-        return carry
-
-    lax.fori_loop(1, n_far + 1, rhs_wait, 0)
+
+    for at, flip, count in broadcast:
+        each(count, lambda i: rhs_wait(at, flip, i))
 
     def chosen(at, x):
         picked = jnp.zeros((8, 128), F32)
@@ -282,90 +331,112 @@
             picked = picked + jnp.where(owner[k] == x, rhs_in[at, k].astype(F32), 0.0)
         return picked
 
-    ahead_x = lax.rem(g + 1, n_group)
-    behind_x = lax.rem(g + n_group - 1, n_group)
+    ahead_x, behind_x = device(1, 0)[0], device(-1, 0)[0]
     rhs = chosen(0, g)
     others = [chosen(0, ahead_x), chosen(0, behind_x), chosen(1, g), chosen(2, g)]
-    iterate = rhs - hop(weights, rhs, others, row)
-
-    steps = [(n_group - 1, 0), (1, 0), (0, n_sub - 1), (0, 1)]
-    pending = []
-    for step in range(COARSE_STEPS - 1):
-        iter_out[step] = iterate
-        copies = [
-            pltpu.make_async_remote_copy(
-                src_ref=iter_out.at[step],
-                dst_ref=iter_in.at[step, way],
-                send_sem=iter_send.at[step, way],
-                recv_sem=iter_recv.at[step, way],
-                device_id=device(*steps[way]),
-                device_id_type=MESH,
-            )
-            for way in range(4)
+    first = rhs - hop(weights, rhs, others, row)
+
+    near_out[0] = first.astype(BF16)
+    near_out[1] = (rhs - hop(weights, first, [], row)).astype(BF16)
+    pushed = pushes(toward, first, row, lane)
+    pairs = [(kx, kt) for kx in (0, 1) for kt in (2, 3)]
+    for at, pair in enumerate(pairs):
+        for side in range(2):
+            skew_out[at, side] = pushed[pair[side]].astype(BF16)
+    for k in range(4):
+        far_out[k] = pushed[k].astype(BF16)
+
+    def back(*ks):
+        return device(-sum(ahead[k][0] for k in ks), -sum(ahead[k][1] for k in ks))
+
+    mid_copies = (
+        [
+            remote(skew_out.at[at], skew_in.at[at], mid_send.at[8 + at], mid_recv.at[8 + at], back(*pair))
+            for at, pair in enumerate(pairs)
         ]
-        for copy in copies:
-            copy.start()
-        for copy in copies:
-            copy.wait_recv()
-        pending += copies
-        iterate = rhs - hop(weights, iterate, [iter_in[step, way] for way in range(4)], row)
-
-    rounded = iterate.astype(BF16)
-    last_out[...] = rounded
-    last_in[g] = rounded
-
-    def last_copy(i, at):
-        return pltpu.make_async_remote_copy(
-            src_ref=last_out,
-            dst_ref=last_in.at[at],
-            send_sem=last_send.at[i],
-            recv_sem=last_recv.at[at],
-            device_id=device(i, 0),
-            device_id_type=MESH,
-        )
-
-    def last_start(i, carry):
-        last_copy(i, g).start()
-        return carry
-
-    lax.fori_loop(1, n_group, last_start, 0)
-    sol_ref[...] = iterate
-
-    def last_wait(i, carry):
-        last_copy(i, lax.rem(g + i, n_group)).wait_recv()
-        return carry
-
-    lax.fori_loop(1, n_group, last_wait, 0)
-
+        + [
+            remote(near_out, near_in.at[k], mid_send.at[k], mid_recv.at[k], back(k))
+            for k in range(4)
+        ]
+        + [
+            remote(far_out.at[k], far_in.at[k], mid_send.at[4 + k], mid_recv.at[4 + k], back(k, k))
+            for k in range(4)
+        ]
+    )
+    for copy in mid_copies:
+        copy.start()
+    for copy in mid_copies:
+        copy.wait_recv()
+    second = rhs - hop(weights, first, [near_in[k, 0].astype(F32) for k in range(4)], row)
+    around = []
+    for k in range(4):
+        value = near_in[k, 1].astype(F32) - far_in[k].astype(F32) - pushed[k ^ 1]
+        for at, pair in enumerate(pairs):
+            if k in pair:
+                value = value - skew_in[at, 1 - pair.index(k)].astype(F32)
+        around.append(value)
+    third = rhs - hop(weights, second, around, row)
+
+    part = rhs - hop(weights, third, [], row)
+    pushed = pushes(toward, third, row, lane)
+    for at, piece in enumerate((part, pushed[0], pushed[1])):
+        last_out[at] = piece.astype(BF16)
+        last_in[g, at] = piece.astype(BF16)
+    turn_out[0] = pushed[2].astype(BF16)
+    turn_out[1] = pushed[3].astype(BF16)
+
+    def last_copy(at, flip, i, source):
+        src = last_out if at == 0 else turn_out.at[at - 1]
+        dst = last_in.at[source] if at == 0 else turn_in.at[at - 1, source]
+        return remote(
+            src,
+            dst,
+            last_send.at[at, flip * half + i],
+            last_recv.at[at, source],
+            (member(flip, i), device(0, to_t[at])[1]),
+        )
+
+    for at, flip, count in broadcast:
+        each(count, lambda i: last_copy(at, flip, i, g).start())
     block_here = jnp.int32(0)
     for k in range(n_group):
         block_here = block_here + jnp.where(g == k, owner[k], 0)
-    own = jnp.zeros((8, 128), F32)
-    for k in range(n_group):
-        own = own + jnp.where(block_here == k, last_in[k].astype(F32), 0.0)
-
-    own_ref[...] = own
-
-    def rhs_done(i, carry):
-        rhs_copy(i).wait_send()
-        return carry
-
-    lax.fori_loop(1, n_far + 1, rhs_done, 0)
-    for copy in pending:
+    for at, flip, count in broadcast:
+        each(count, lambda i: last_copy(at, flip, i, member(flip, i)).wait_recv())
+
+    def gathered(start, x):
+        after, before = lax.rem(x + 1, n_group), lax.rem(x + n_group - 1, n_group)
+        value = start
+        for k in range(n_group):
+            if start is None:
+                mine = last_in[k, 0].astype(F32)
+                mine = mine - turn_in[0, k].astype(F32) - turn_in[1, k].astype(F32)
+                value = jnp.where(x == k, mine, 0.0) + (0.0 if value is None else value)
+            else:
+                mine = turn_in[0, k].astype(F32) + turn_in[1, k].astype(F32)
+                value = value - jnp.where(x == k, mine, 0.0)
+            value = value - jnp.where(after == k, last_in[k, 1].astype(F32), 0.0)
+            value = value - jnp.where(before == k, last_in[k, 2].astype(F32), 0.0)
+        return value
+
+    sol_ref[...] = gathered(part, g)
+    own_ref[...] = gathered(None, block_here).astype(BF16).astype(F32)
+
+    for copy in link_copies + mid_copies:
         copy.wait_send()
-
-    def last_done(i, carry):
-        last_copy(i, g).wait_send()
-        return carry
-
-    lax.fori_loop(1, n_group, last_done, 0)
+    for at, flip, count in broadcast:
+        each(count, lambda i: rhs_copy(at, flip, i).wait_send())
+        each(count, lambda i: last_copy(at, flip, i, g).wait_send())
 
 
 def on_device(n_group, n_sub, fine_residual, null_vectors, agg_map, block_owner, coarse_links):
     hbm = pl.BlockSpec(memory_space=pltpu.HBM)
     vmem = pl.BlockSpec(memory_space=pltpu.VMEM)
     dma = pltpu.SemaphoreType.DMA
-    exchanges = COARSE_STEPS - 1
+
+    def piece(*lead):
+        return pltpu.VMEM((*lead, 8, 128), BF16)
+
     in_hbm = functools.partial(pltpu.with_memory_space_constraint, memory_space=pltpu.HBM)
     solved = pl.pallas_call(
         functools.partial(kernel, n_group, n_sub),
@@ -383,19 +454,30 @@
             pltpu.VMEM((36, CDOF, CDOF), BF16),
             pltpu.SMEM((n_group,), jnp.int32),
             pltpu.VMEM((6 * 128, 256), BF16),
-            pltpu.VMEM((8, 128), BF16),
-            pltpu.VMEM((3, n_group, 8, 128), BF16),
-            pltpu.VMEM((exchanges, 8, 128), F32),
-            pltpu.VMEM((exchanges, 4, 8, 128), F32),
-            pltpu.VMEM((8, 128), BF16),
-            pltpu.VMEM((n_group, 8, 128), BF16),
+            pltpu.VMEM((128, 4 * 128), BF16),
+            pltpu.VMEM((4, 128, 128), BF16),
+            pltpu.VMEM((4, 128, 128), BF16),
+            piece(),
+            piece(3, n_group),
+            piece(2),
+            piece(4, 2),
+            piece(4),
+            piece(4),
+            piece(4, 2),
+            piece(4, 2),
+            piece(3),
+            piece(n_group, 3),
+            piece(2),
+            piece(2, n_group),
             dma((4 + NBLOCK,)),
-            dma((3 * n_group,)),
+            dma((4,)),
+            dma((4,)),
             dma((3, n_group)),
-            dma((exchanges, 4)),
-            dma((exchanges, 4)),
-            dma((n_group,)),
-            dma((n_group,)),
+            dma((3, n_group)),
+            dma((12,)),
+            dma((12,)),
+            dma((3, n_group)),
+            dma((3, n_group)),
         ],
         compiler_params=pltpu.CompilerParams(
             collective_id=0, has_side_effects=True, vmem_limit_bytes=24 * 1024 * 1024

time: 50.2 us -> 44.8 us (0.89)
  Pallas kernels: 49.4 us -> 44 us
    pallas_call x1, Pallas kernels: 48.2 us -> 42.8 us  [on_device(): pl.pallas_call(functools.partial(kernel, n_group, n_sub), out_shape=(jax....]
where the time goes in v3:
time: 44.8 us; the launch traced here: 44.6 us
  Pallas kernels  44 us (98%)
  between operations  0.64 us (1%)
    pallas_call x1, Pallas kernels, on_device(): pl.pallas_call(functools.partial(kernel, n_group, n_sub), out_shape=(jax....  42.8 us
    pallas_call x1, Pallas kernels, on_device(): pl.pallas_call(prolong_kernel, out_shape=(jax.ShapeDtypeStruct((2, 2, RHS...  1.17 us

profile of v3, /device:TPU:1, one launch (start us, length us, event | category | flops | bytes accessed | tf_op | source)
XLA Modules:
  0.0 44.6 jit_solution(15029754665382717740)
XLA Ops:
  0.6 42.8 %coarse.1 = (f32[8,128]{1,0:T(8,128)S(1)}, f32[8,128]{1,0:T(8,128)S(1)}, f32[4,1024]{1,0:T(4,128)S(1)}, bf16[2,12,32,1024]{3,2,1,0:T(8,128)(2,1)S(1)}) custom-call(s32[16]{0:T(128)} %owner_ref.1, bf16[2,12,4,1024]{3,2,1,0:T(4,128)(2,1)} %fine_ref.1, bf16[2,12,32,1024]{3,2,1,0:T(8,128)(2,1)} %null_ref.1, s32[1,1024]{1,0:T(1,128)} %agg_ref.1, ...), custom_call_target="tpu_custom_call" | custom-call | tf_op jit(solution)/shard_map/coarse/pallas_call | solution.py:441
  43.4 1.2 %prolong.1 = (f32[2,2,4,64]{3,2,1,0:T(4,128)}, bf16[2,12,4,1024]{3,2,1,0:T(4,128)(2,1)}) custom-call(f32[8,128]{1,0:T(8,128)S(1)} %get-tuple-element.8.sol_ref, f32[8,128]{1,0:T(8,128)S(1)} %get-tuple-element.9.own_ref, f32[4,1024]{1,0:T(4,128)S(1)} %get-tuple-element.10.masks_ref, bf16[2,12,32,1024]{3,2,1,0:T(8,128)(2,1)S(1)} %get-tuple-element.11.null), custom_call_target="tpu_custom_call" | custom-call | tf_op jit(solution)/shard_map/prolong/pallas_call | solution.py:493

commit v4 on v3

--- a/solution.py
+++ b/solution.py
@@ -191,11 +191,9 @@
     rhs_out,
     rhs_in,
     near_out,
-    near_in,
     far_out,
-    far_in,
     skew_out,
-    skew_in,
+    mid_in,
     last_out,
     last_in,
     turn_out,
@@ -209,6 +207,8 @@
     mid_recv,
     last_send,
     last_recv,
+    turn_send,
+    turn_recv,
 ):
     g = lax.axis_index("group")
     s = lax.axis_index("sub")
@@ -229,11 +229,11 @@
         )
 
     def each(count, body):
-        def run(i, carry):
+        for i in range(count):
             body(i)
-            return carry
-
-        lax.fori_loop(0, count, run, 0)
+
+    def arrived(buffer, sem):
+        pltpu.make_async_copy(buffer, buffer, sem).wait()
 
     load_agg = pltpu.make_async_copy(agg_ref, agg, local_sem.at[0])
     load_fine = pltpu.make_async_copy(fine_ref, fine, local_sem.at[1])
@@ -247,25 +247,25 @@
         for b in range(NBLOCK)
     ]
     load_owner = pltpu.make_async_copy(owner_ref, owner, local_sem.at[3 + NBLOCK])
+    to_t = (0, -1, 1)
+    barrier = pltpu.get_barrier_semaphore()
+
+    def greet(to):
+        pl.semaphore_signal(barrier, inc=1, device_id=to, device_id_type=MESH)
+
+    for flip in (1, 0):
+        for at in (2, 1, 0):
+            count = half - 1 if at == 0 and flip == 0 else half
+            each(count, lambda i: greet((member(flip, i), device(0, to_t[at])[1])))
+    greet(device(0, 2))
+    greet(device(0, -2))
+
     load_agg.start()
     load_fine.start()
     for load in load_null:
         load.start()
     load_links.start()
     load_owner.start()
-
-    to_t = (0, -1, 1)
-    barrier = pltpu.get_barrier_semaphore()
-
-    def greet(to):
-        pl.semaphore_signal(barrier, inc=1, device_id=to, device_id_type=MESH)
-
-    for at in (2, 1, 0):
-        for flip in (1, 0):
-            count = half - 1 if at == 0 and flip == 0 else half
-            each(count, lambda i: greet((member(flip, i), device(0, to_t[at])[1])))
-    greet(device(0, 2))
-    greet(device(0, -2))
 
     row = lax.broadcasted_iota(jnp.int32, (8, 128), 0)
     lane = lax.broadcasted_iota(jnp.int32, (8, 128), 1)
@@ -277,7 +277,8 @@
     load_fine.wait()
     mine = restrict(fine, null, masks, row, lane, load_null).astype(BF16)
     rhs_out[...] = mine
-    rhs_in[0, g] = mine
+    keep_rhs = pltpu.make_async_copy(rhs_out, rhs_in.at[0, g], rhs_recv)
+    keep_rhs.start()
 
     pl.semaphore_wait(barrier, 3 * n_group - 1 + 2)
 
@@ -285,8 +286,8 @@
         return remote(
             rhs_out,
             rhs_in.at[at, g],
-            rhs_send.at[at, flip * half + i],
-            rhs_recv.at[at, g],
+            rhs_send,
+            rhs_recv,
             (member(flip, i), device(0, to_t[at])[1]),
         )
 
@@ -298,7 +299,6 @@
 
     ahead = ((1, 0), (-1, 0), (0, 1), (0, -1))
     load_links.wait()
-    link_copies = []
     for k in range(4):
         for y in range(2):
             at = (k + 1) * 4 + 2 * y
@@ -306,24 +306,16 @@
                 [links[at], links[at + 1]], axis=1
             )
         copy = remote(
-            link_out.at[k], link_in.at[k], link_send.at[k], link_recv.at[k], device(*ahead[k])
+            link_out.at[k], link_in.at[k], link_send, link_recv, device(*ahead[k])
         )
         copy.start()
-        link_copies.append(copy)
     build_operator(links, weights)
     load_owner.wait()
-    for k, copy in enumerate(link_copies):
-        copy.wait_recv()
+    arrived(link_in, link_recv)
+    for k in range(4):
         toward[:, k * 128 : (k + 1) * 128] = link_in[k].T
 
-    def rhs_wait(at, flip, i):
-        source = member(flip, i)
-        remote(
-            rhs_out, rhs_in.at[at, source], rhs_send.at[at, 0], rhs_recv.at[at, source], device(0, 1)
-        ).wait_recv()
-
-    for at, flip, count in broadcast:
-        each(count, lambda i: rhs_wait(at, flip, i))
+    arrived(rhs_in, rhs_recv)
 
     def chosen(at, x):
         picked = jnp.zeros((8, 128), F32)
@@ -351,29 +343,28 @@
 
     mid_copies = (
         [
-            remote(skew_out.at[at], skew_in.at[at], mid_send.at[8 + at], mid_recv.at[8 + at], back(*pair))
+            remote(skew_out.at[at], mid_in.at[pl.ds(12 + 2 * at, 2)], mid_send, mid_recv, back(*pair))
             for at, pair in enumerate(pairs)
         ]
         + [
-            remote(near_out, near_in.at[k], mid_send.at[k], mid_recv.at[k], back(k))
+            remote(near_out, mid_in.at[pl.ds(2 * k, 2)], mid_send, mid_recv, back(k))
             for k in range(4)
         ]
         + [
-            remote(far_out.at[k], far_in.at[k], mid_send.at[4 + k], mid_recv.at[4 + k], back(k, k))
+            remote(far_out.at[k], mid_in.at[8 + k], mid_send, mid_recv, back(k, k))
             for k in range(4)
         ]
     )
     for copy in mid_copies:
         copy.start()
-    for copy in mid_copies:
-        copy.wait_recv()
-    second = rhs - hop(weights, first, [near_in[k, 0].astype(F32) for k in range(4)], row)
+    arrived(mid_in, mid_recv)
+    second = rhs - hop(weights, first, [mid_in[2 * k].astype(F32) for k in range(4)], row)
     around = []
     for k in range(4):
-        value = near_in[k, 1].astype(F32) - far_in[k].astype(F32) - pushed[k ^ 1]
+        value = mid_in[2 * k + 1].astype(F32) - mid_in[8 + k].astype(F32) - pushed[k ^ 1]
         for at, pair in enumerate(pairs):
             if k in pair:
-                value = value - skew_in[at, 1 - pair.index(k)].astype(F32)
+                value = value - mid_in[12 + 2 * at + 1 - pair.index(k)].astype(F32)
         around.append(value)
     third = rhs - hop(weights, second, around, row)
 
@@ -381,28 +372,29 @@
     pushed = pushes(toward, third, row, lane)
     for at, piece in enumerate((part, pushed[0], pushed[1])):
         last_out[at] = piece.astype(BF16)
-        last_in[g, at] = piece.astype(BF16)
+    keep_last = pltpu.make_async_copy(last_out, last_in.at[g], last_recv)
+    keep_last.start()
     turn_out[0] = pushed[2].astype(BF16)
     turn_out[1] = pushed[3].astype(BF16)
 
-    def last_copy(at, flip, i, source):
+    def last_copy(at, flip, i):
         src = last_out if at == 0 else turn_out.at[at - 1]
-        dst = last_in.at[source] if at == 0 else turn_in.at[at - 1, source]
+        dst = last_in.at[g] if at == 0 else turn_in.at[at - 1, g]
         return remote(
             src,
             dst,
-            last_send.at[at, flip * half + i],
-            last_recv.at[at, source],
+            last_send if at == 0 else turn_send,
+            last_recv if at == 0 else turn_recv,
             (member(flip, i), device(0, to_t[at])[1]),
         )
 
     for at, flip, count in broadcast:
-        each(count, lambda i: last_copy(at, flip, i, g).start())
+        each(count, lambda i: last_copy(at, flip, i).start())
     block_here = jnp.int32(0)
     for k in range(n_group):
         block_here = block_here + jnp.where(g == k, owner[k], 0)
-    for at, flip, count in broadcast:
-        each(count, lambda i: last_copy(at, flip, i, member(flip, i)).wait_recv())
+    arrived(last_in, last_recv)
+    arrived(turn_in, turn_recv)
 
     def gathered(start, x):
         after, before = lax.rem(x + 1, n_group), lax.rem(x + n_group - 1, n_group)
@@ -422,11 +414,12 @@
     sol_ref[...] = gathered(part, g)
     own_ref[...] = gathered(None, block_here).astype(BF16).astype(F32)
 
-    for copy in link_copies + mid_copies:
-        copy.wait_send()
-    for at, flip, count in broadcast:
-        each(count, lambda i: rhs_copy(at, flip, i).wait_send())
-        each(count, lambda i: last_copy(at, flip, i, g).wait_send())
+    arrived(rhs_in.at[pl.ds(0, 2)], rhs_send)
+    arrived(rhs_in.at[2, pl.ds(0, n_group - 1)], rhs_send)
+    arrived(link_in, link_send)
+    arrived(mid_in, mid_send)
+    arrived(last_in.at[pl.ds(0, n_group - 1)], last_send)
+    arrived(turn_in, turn_send)
 
 
 def on_device(n_group, n_sub, fine_residual, null_vectors, agg_map, block_owner, coarse_links):
@@ -460,25 +453,16 @@
             piece(),
             piece(3, n_group),
             piece(2),
-            piece(4, 2),
-            piece(4),
             piece(4),
             piece(4, 2),
-            piece(4, 2),
+            piece(20),
             piece(3),
             piece(n_group, 3),
             piece(2),
             piece(2, n_group),
             dma((4 + NBLOCK,)),
-            dma((4,)),
-            dma((4,)),
-            dma((3, n_group)),
-            dma((3, n_group)),
-            dma((12,)),
-            dma((12,)),
-            dma((3, n_group)),
-            dma((3, n_group)),
-        ],
+        ]
+        + [dma] * 10,
         compiler_params=pltpu.CompilerParams(
             collective_id=0, has_side_effects=True, vmem_limit_bytes=24 * 1024 * 1024
         ),

time: 44.8 us -> 41.1 us (0.917)
  the two profiles are of different devices: /device:TPU:1 before, /device:TPU:17 now
where the time goes in v4:
time: 41.1 us; the launch traced here: 40.9 us
  Pallas kernels  40.3 us (98%)
  between operations  0.64 us (2%)
    pallas_call x1, Pallas kernels, on_device(): pl.pallas_call(functools.partial(kernel, n_group, n_sub), out_shape=(jax....  39.1 us
    pallas_call x1, Pallas kernels, on_device(): pl.pallas_call(prolong_kernel, out_shape=(jax.ShapeDtypeStruct((2, 2, RHS...  1.17 us

profile of v4, /device:TPU:17, one launch (start us, length us, event | category | flops | bytes accessed | tf_op | source)
XLA Modules:
  0.0 40.9 jit_solution(13506012777077387855)
XLA Ops:
  0.6 39.1 %coarse.1 = (f32[8,128]{1,0:T(8,128)S(1)}, f32[8,128]{1,0:T(8,128)S(1)}, f32[4,1024]{1,0:T(4,128)S(1)}, bf16[2,12,32,1024]{3,2,1,0:T(8,128)(2,1)S(1)}) custom-call(s32[16]{0:T(128)} %owner_ref.1, bf16[2,12,4,1024]{3,2,1,0:T(4,128)(2,1)} %fine_ref.1, bf16[2,12,32,1024]{3,2,1,0:T(8,128)(2,1)} %null_ref.1, s32[1,1024]{1,0:T(1,128)} %agg_ref.1, ...), custom_call_target="tpu_custom_call" | custom-call | tf_op jit(solution)/shard_map/coarse/pallas_call | solution.py:434
  39.8 1.2 %prolong.1 = (f32[2,2,4,64]{3,2,1,0:T(4,128)}, bf16[2,12,4,1024]{3,2,1,0:T(4,128)(2,1)}) custom-call(f32[8,128]{1,0:T(8,128)S(1)} %get-tuple-element.8.sol_ref, f32[8,128]{1,0:T(8,128)S(1)} %get-tuple-element.9.own_ref, f32[4,1024]{1,0:T(4,128)S(1)} %get-tuple-element.10.masks_ref, bf16[2,12,32,1024]{3,2,1,0:T(8,128)(2,1)S(1)} %get-tuple-element.11.null), custom_call_target="tpu_custom_call" | custom-call | tf_op jit(solution)/shard_map/prolong/pallas_call | solution.py:477

commit v5 on v4

--- a/solution.py
+++ b/solution.py
@@ -149,11 +149,15 @@
                 weights[source * 128 : (source + 1) * 128, n * CDOF : (n + 1) * CDOF] = column.T
 
 
-def hop(weights, here, others, row):
-    low = [here, pltpu.roll(here, 4, 0)] + list(others)
-    low = jnp.concatenate(low, axis=1).astype(BF16)
-    out = jnp.dot(low, weights[: len(others) * 128 + 256], preferred_element_type=F32)
+def hop(weights, pieces, start, row):
+    low = jnp.concatenate(pieces, axis=1).astype(BF16)
+    rows = weights[start * 128 : (start + len(pieces)) * 128]
+    out = jnp.dot(low, rows, preferred_element_type=F32)
     return jnp.where(row < 4, out[:, :128], out[:, 128:])
+
+
+def here_twice(here):
+    return [here, pltpu.roll(here, 4, 0)]
 
 
 def pushes(toward, here, row, lane):
@@ -187,10 +191,10 @@
     weights,
     toward,
     link_out,
-    link_in,
     rhs_out,
     rhs_in,
     near_out,
+    near_in,
     far_out,
     skew_out,
     mid_in,
@@ -203,6 +207,8 @@
     link_recv,
     rhs_send,
     rhs_recv,
+    near_send,
+    near_recv,
     mid_send,
     mid_recv,
     last_send,
@@ -277,8 +283,17 @@
     load_fine.wait()
     mine = restrict(fine, null, masks, row, lane, load_null).astype(BF16)
     rhs_out[...] = mine
-    keep_rhs = pltpu.make_async_copy(rhs_out, rhs_in.at[0, g], rhs_recv)
+    keep_rhs = pltpu.make_async_copy(rhs_out, rhs_in.at[0, g], rhs_recv.at[0])
     keep_rhs.start()
+
+    ahead = ((1, 0), (-1, 0), (0, 1), (0, -1))
+    load_links.wait()
+    for k in range(4):
+        at = (k + 1) * 4
+        rows = [
+            jnp.concatenate([links[at + 2 * y], links[at + 2 * y + 1]], axis=1) for y in range(2)
+        ]
+        link_out[k] = jnp.concatenate(rows, axis=0).T
 
     pl.semaphore_wait(barrier, 3 * n_group - 1 + 2)
 
@@ -287,7 +302,7 @@
             rhs_out,
             rhs_in.at[at, g],
             rhs_send,
-            rhs_recv,
+            rhs_recv.at[at],
             (member(flip, i), device(0, to_t[at])[1]),
         )
 
@@ -297,25 +312,16 @@
     for at, flip, count in broadcast:
         each(count, lambda i: rhs_copy(at, flip, i).start())
 
-    ahead = ((1, 0), (-1, 0), (0, 1), (0, -1))
-    load_links.wait()
-    for k in range(4):
-        for y in range(2):
-            at = (k + 1) * 4 + 2 * y
-            link_out[k, y * CDOF : (y + 1) * CDOF] = jnp.concatenate(
-                [links[at], links[at + 1]], axis=1
-            )
-        copy = remote(
-            link_out.at[k], link_in.at[k], link_send, link_recv, device(*ahead[k])
-        )
-        copy.start()
+    for k in range(4):
+        remote(
+            link_out.at[k],
+            toward.at[:, pl.ds(k * 128, 128)],
+            link_send,
+            link_recv,
+            device(*ahead[k]),
+        ).start()
     build_operator(links, weights)
     load_owner.wait()
-    arrived(link_in, link_recv)
-    for k in range(4):
-        toward[:, k * 128 : (k + 1) * 128] = link_in[k].T
-
-    arrived(rhs_in, rhs_recv)
 
     def chosen(at, x):
         picked = jnp.zeros((8, 128), F32)
@@ -323,102 +329,98 @@
             picked = picked + jnp.where(owner[k] == x, rhs_in[at, k].astype(F32), 0.0)
         return picked
 
-    ahead_x, behind_x = device(1, 0)[0], device(-1, 0)[0]
+    after, before = device(1, 0)[0], device(-1, 0)[0]
+    arrived(rhs_in.at[0], rhs_recv.at[0])
     rhs = chosen(0, g)
-    others = [chosen(0, ahead_x), chosen(0, behind_x), chosen(1, g), chosen(2, g)]
-    first = rhs - hop(weights, rhs, others, row)
-
+    side = [chosen(0, after), chosen(0, before)]
+    first = rhs - hop(weights, here_twice(rhs) + side, 0, row)
+    for at in (1, 2):
+        arrived(rhs_in.at[at], rhs_recv.at[at])
+    first = first - hop(weights, [chosen(1, g), chosen(2, g)], 4, row)
+
+    def back(*ks):
+        return device(-sum(ahead[k][0] for k in ks), -sum(ahead[k][1] for k in ks))
+
+    part = rhs - hop(weights, here_twice(first), 0, row)
     near_out[0] = first.astype(BF16)
-    near_out[1] = (rhs - hop(weights, first, [], row)).astype(BF16)
+    near_out[1] = part.astype(BF16)
+    for k in range(4):
+        remote(near_out, near_in.at[pl.ds(2 * k, 2)], near_send, near_recv, back(k)).start()
+    arrived(toward, link_recv)
     pushed = pushes(toward, first, row, lane)
     pairs = [(kx, kt) for kx in (0, 1) for kt in (2, 3)]
     for at, pair in enumerate(pairs):
-        for side in range(2):
-            skew_out[at, side] = pushed[pair[side]].astype(BF16)
+        for k in range(2):
+            skew_out[at, k] = pushed[pair[k]].astype(BF16)
+        remote(skew_out.at[at], mid_in.at[pl.ds(4 + 2 * at, 2)], mid_send, mid_recv, back(*pair)).start()
     for k in range(4):
         far_out[k] = pushed[k].astype(BF16)
-
-    def back(*ks):
-        return device(-sum(ahead[k][0] for k in ks), -sum(ahead[k][1] for k in ks))
-
-    mid_copies = (
-        [
-            remote(skew_out.at[at], mid_in.at[pl.ds(12 + 2 * at, 2)], mid_send, mid_recv, back(*pair))
-            for at, pair in enumerate(pairs)
-        ]
-        + [
-            remote(near_out, mid_in.at[pl.ds(2 * k, 2)], mid_send, mid_recv, back(k))
-            for k in range(4)
-        ]
-        + [
-            remote(far_out.at[k], mid_in.at[8 + k], mid_send, mid_recv, back(k, k))
-            for k in range(4)
-        ]
-    )
-    for copy in mid_copies:
-        copy.start()
+        remote(far_out.at[k], mid_in.at[k], mid_send, mid_recv, back(k, k)).start()
+
+    arrived(near_in, near_recv)
+    second = part - hop(weights, [near_in[2 * k].astype(F32) for k in range(4)], 2, row)
+    third = rhs - hop(weights, here_twice(second), 0, row)
+    known = [near_in[2 * k + 1].astype(F32) - pushed[k ^ 1] for k in range(4)]
     arrived(mid_in, mid_recv)
-    second = rhs - hop(weights, first, [mid_in[2 * k].astype(F32) for k in range(4)], row)
     around = []
     for k in range(4):
-        value = mid_in[2 * k + 1].astype(F32) - mid_in[8 + k].astype(F32) - pushed[k ^ 1]
+        value = known[k] - mid_in[k].astype(F32)
         for at, pair in enumerate(pairs):
             if k in pair:
-                value = value - mid_in[12 + 2 * at + 1 - pair.index(k)].astype(F32)
+                value = value - mid_in[4 + 2 * at + 1 - pair.index(k)].astype(F32)
         around.append(value)
-    third = rhs - hop(weights, second, around, row)
-
-    part = rhs - hop(weights, third, [], row)
+    third = third - hop(weights, around, 2, row)
+
+    part = rhs - hop(weights, here_twice(third), 0, row)
     pushed = pushes(toward, third, row, lane)
-    for at, piece in enumerate((part, pushed[0], pushed[1])):
-        last_out[at] = piece.astype(BF16)
-    keep_last = pltpu.make_async_copy(last_out, last_in.at[g], last_recv)
+
+    def wanted(at, place):
+        block = owner[place]
+        if at:
+            return jnp.where(block == g, pushed[1 + at], 0.0)
+        piece = jnp.where(block == g, part, 0.0)
+        return piece - jnp.where(block == before, pushed[0], jnp.where(block == after, pushed[1], 0.0))
+
+    for at, flip, count in broadcast:
+        for i in range(count):
+            place = member(flip, i)
+            slot = at * n_group + flip * half + i
+            last_out[slot] = wanted(at, place).astype(BF16)
+            remote(
+                last_out.at[slot],
+                last_in.at[at * n_group + g],
+                last_send,
+                last_recv,
+                (place, device(0, to_t[at])[1]),
+            ).start()
+    for k in range(4):
+        turn_out[k] = pushed[k].astype(BF16)
+        remote(turn_out.at[k], turn_in.at[k], turn_send, turn_recv, back(k)).start()
+    kept = wanted(0, g).astype(BF16)
+    last_out[half - 1] = kept
+    keep_last = pltpu.make_async_copy(last_out.at[half - 1], last_in.at[g], last_recv)
     keep_last.start()
-    turn_out[0] = pushed[2].astype(BF16)
-    turn_out[1] = pushed[3].astype(BF16)
-
-    def last_copy(at, flip, i):
-        src = last_out if at == 0 else turn_out.at[at - 1]
-        dst = last_in.at[g] if at == 0 else turn_in.at[at - 1, g]
-        return remote(
-            src,
-            dst,
-            last_send if at == 0 else turn_send,
-            last_recv if at == 0 else turn_recv,
-            (member(flip, i), device(0, to_t[at])[1]),
-        )
-
-    for at, flip, count in broadcast:
-        each(count, lambda i: last_copy(at, flip, i).start())
-    block_here = jnp.int32(0)
-    for k in range(n_group):
-        block_here = block_here + jnp.where(g == k, owner[k], 0)
+
+    arrived(turn_in, turn_recv)
+    whole = part
+    for k in range(4):
+        whole = whole - turn_in[k].astype(F32)
+    sol_ref[...] = whole
     arrived(last_in, last_recv)
-    arrived(turn_in, turn_recv)
-
-    def gathered(start, x):
-        after, before = lax.rem(x + 1, n_group), lax.rem(x + n_group - 1, n_group)
-        value = start
-        for k in range(n_group):
-            if start is None:
-                mine = last_in[k, 0].astype(F32)
-                mine = mine - turn_in[0, k].astype(F32) - turn_in[1, k].astype(F32)
-                value = jnp.where(x == k, mine, 0.0) + (0.0 if value is None else value)
-            else:
-                mine = turn_in[0, k].astype(F32) + turn_in[1, k].astype(F32)
-                value = value - jnp.where(x == k, mine, 0.0)
-            value = value - jnp.where(after == k, last_in[k, 1].astype(F32), 0.0)
-            value = value - jnp.where(before == k, last_in[k, 2].astype(F32), 0.0)
-        return value
-
-    sol_ref[...] = gathered(part, g)
-    own_ref[...] = gathered(None, block_here).astype(BF16).astype(F32)
+    own = last_in[0].astype(F32)
+    for k in range(1, n_group):
+        own = own + last_in[k].astype(F32)
+    turned = last_in[n_group].astype(F32)
+    for k in range(n_group + 1, 3 * n_group):
+        turned = turned + last_in[k].astype(F32)
+    own_ref[...] = (own - turned).astype(BF16).astype(F32)
 
     arrived(rhs_in.at[pl.ds(0, 2)], rhs_send)
     arrived(rhs_in.at[2, pl.ds(0, n_group - 1)], rhs_send)
-    arrived(link_in, link_send)
+    arrived(toward, link_send)
+    arrived(near_in, near_send)
     arrived(mid_in, mid_send)
-    arrived(last_in.at[pl.ds(0, n_group - 1)], last_send)
+    arrived(last_in.at[pl.ds(0, 3 * n_group - 1)], last_send)
     arrived(turn_in, turn_send)
 
 
@@ -449,20 +451,24 @@
             pltpu.VMEM((6 * 128, 256), BF16),
             pltpu.VMEM((128, 4 * 128), BF16),
             pltpu.VMEM((4, 128, 128), BF16),
-            pltpu.VMEM((4, 128, 128), BF16),
             piece(),
             piece(3, n_group),
             piece(2),
+            piece(8),
             piece(4),
             piece(4, 2),
-            piece(20),
-            piece(3),
-            piece(n_group, 3),
-            piece(2),
-            piece(2, n_group),
+            piece(12),
+            piece(3 * n_group),
+            piece(3 * n_group),
+            piece(4),
+            piece(4),
             dma((4 + NBLOCK,)),
+            dma,
+            dma,
+            dma,
+            dma((3,)),
         ]
-        + [dma] * 10,
+        + [dma] * 8,
         compiler_params=pltpu.CompilerParams(
             collective_id=0, has_side_effects=True, vmem_limit_bytes=24 * 1024 * 1024
         ),

time: 41.1 us -> 39.7 us (0.966)
  the two profiles are of different devices: /device:TPU:17 before, /device:TPU:1 now
where the time goes in v5:
time: 39.7 us; the launch traced here: 39.5 us
  Pallas kernels  38.9 us (98%)
  between operations  0.64 us (2%)
    pallas_call x1, Pallas kernels, on_device(): pl.pallas_call(functools.partial(kernel, n_group, n_sub), out_shape=(jax....  37.7 us
    pallas_call x1, Pallas kernels, on_device(): pl.pallas_call(prolong_kernel, out_shape=(jax.ShapeDtypeStruct((2, 2, RHS...  1.17 us

profile of v5, /device:TPU:1, one launch (start us, length us, event | category | flops | bytes accessed | tf_op | source)
XLA Modules:
  0.0 39.5 jit_solution(3414160942532171273)
XLA Ops:
  0.6 37.7 %coarse.1 = (f32[8,128]{1,0:T(8,128)S(1)}, f32[8,128]{1,0:T(8,128)S(1)}, f32[4,1024]{1,0:T(4,128)S(1)}, bf16[2,12,32,1024]{3,2,1,0:T(8,128)(2,1)S(1)}) custom-call(s32[16]{0:T(128)} %owner_ref.1, bf16[2,12,4,1024]{3,2,1,0:T(4,128)(2,1)} %fine_ref.1, bf16[2,12,32,1024]{3,2,1,0:T(8,128)(2,1)} %null_ref.1, s32[1,1024]{1,0:T(1,128)} %agg_ref.1, ...), custom_call_target="tpu_custom_call" | custom-call | tf_op jit(solution)/shard_map/coarse/pallas_call | solution.py:436
  38.4 1.2 %prolong.1 = (f32[2,2,4,64]{3,2,1,0:T(4,128)}, bf16[2,12,4,1024]{3,2,1,0:T(4,128)(2,1)}) custom-call(f32[8,128]{1,0:T(8,128)S(1)} %get-tuple-element.8.sol_ref, f32[8,128]{1,0:T(8,128)S(1)} %get-tuple-element.9.own_ref, f32[4,1024]{1,0:T(4,128)S(1)} %get-tuple-element.10.masks_ref, bf16[2,12,32,1024]{3,2,1,0:T(8,128)(2,1)S(1)} %get-tuple-element.11.null), custom_call_target="tpu_custom_call" | custom-call | tf_op jit(solution)/shard_map/prolong/pallas_call | solution.py:483

commit v6 on v5

--- a/solution.py
+++ b/solution.py
@@ -110,14 +110,17 @@
             sol[y, z] = sol_ref[y * RHS : (y + 1) * RHS, z * CDOF : (z + 1) * CDOF]
     stores = [pltpu.make_async_copy(sol, sol_out, sem.at[NBLOCK])]
     stores[0].start()
+    inside = [
+        jnp.broadcast_to(masks_ref[a : a + 1], (32, FS)) > 0.5 for a in range(1, NAGG)
+    ]
     left = prolongation_rows(own_ref[...], row, lane)
     for b in range(NBLOCK):
         at_f = pl.ds(b * FBLOCK, FBLOCK)
         part = null[:, b * FBLOCK : (b + 1) * FBLOCK].reshape(2 * FBLOCK * NULLV, FS)
         wide = jnp.dot(left, part, preferred_element_type=F32)
-        here = wide[:32] * masks_ref[0:1]
+        here = wide[:32]
         for a in range(1, NAGG):
-            here = here + wide[a * 32 : (a + 1) * 32] * masks_ref[a : a + 1]
+            here = jnp.where(inside[a - 1], wide[a * 32 : (a + 1) * 32], here)
         for ri in range(2):
             for f in range(FBLOCK):
                 at = (ri * FBLOCK + f) * RHS
@@ -341,11 +344,6 @@
     def back(*ks):
         return device(-sum(ahead[k][0] for k in ks), -sum(ahead[k][1] for k in ks))
 
-    part = rhs - hop(weights, here_twice(first), 0, row)
-    near_out[0] = first.astype(BF16)
-    near_out[1] = part.astype(BF16)
-    for k in range(4):
-        remote(near_out, near_in.at[pl.ds(2 * k, 2)], near_send, near_recv, back(k)).start()
     arrived(toward, link_recv)
     pushed = pushes(toward, first, row, lane)
     pairs = [(kx, kt) for kx in (0, 1) for kt in (2, 3)]
@@ -356,6 +354,12 @@
     for k in range(4):
         far_out[k] = pushed[k].astype(BF16)
         remote(far_out.at[k], mid_in.at[k], mid_send, mid_recv, back(k, k)).start()
+
+    part = rhs - hop(weights, here_twice(first), 0, row)
+    near_out[0] = first.astype(BF16)
+    near_out[1] = part.astype(BF16)
+    for k in range(4):
+        remote(near_out, near_in.at[pl.ds(2 * k, 2)], near_send, near_recv, back(k)).start()
 
     arrived(near_in, near_recv)
     second = part - hop(weights, [near_in[2 * k].astype(F32) for k in range(4)], 2, row)
@@ -390,7 +394,7 @@
                 last_out.at[slot],
                 last_in.at[at * n_group + g],
                 last_send,
-                last_recv,
+                last_recv.at[at],
                 (place, device(0, to_t[at])[1]),
             ).start()
     for k in range(4):
@@ -398,7 +402,7 @@
         remote(turn_out.at[k], turn_in.at[k], turn_send, turn_recv, back(k)).start()
     kept = wanted(0, g).astype(BF16)
     last_out[half - 1] = kept
-    keep_last = pltpu.make_async_copy(last_out.at[half - 1], last_in.at[g], last_recv)
+    keep_last = pltpu.make_async_copy(last_out.at[half - 1], last_in.at[g], last_recv.at[0])
     keep_last.start()
 
     arrived(turn_in, turn_recv)
@@ -406,14 +410,14 @@
     for k in range(4):
         whole = whole - turn_in[k].astype(F32)
     sol_ref[...] = whole
-    arrived(last_in, last_recv)
-    own = last_in[0].astype(F32)
-    for k in range(1, n_group):
-        own = own + last_in[k].astype(F32)
-    turned = last_in[n_group].astype(F32)
-    for k in range(n_group + 1, 3 * n_group):
-        turned = turned + last_in[k].astype(F32)
-    own_ref[...] = (own - turned).astype(BF16).astype(F32)
+    sums = []
+    for at in range(3):
+        arrived(last_in.at[pl.ds(at * n_group, n_group)], last_recv.at[at])
+        parts = [last_in[at * n_group + k].astype(F32) for k in range(n_group)]
+        while len(parts) > 1:
+            parts = [parts[i] + parts[i + 1] for i in range(0, len(parts), 2)]
+        sums.append(parts[0])
+    own_ref[...] = (sums[0] - sums[1] - sums[2]).astype(BF16).astype(F32)
 
     arrived(rhs_in.at[pl.ds(0, 2)], rhs_send)
     arrived(rhs_in.at[2, pl.ds(0, n_group - 1)], rhs_send)
@@ -468,7 +472,8 @@
             dma,
             dma((3,)),
         ]
-        + [dma] * 8,
+        + [dma] * 5
+        + [dma((3,)), dma, dma],
         compiler_params=pltpu.CompilerParams(
             collective_id=0, has_side_effects=True, vmem_limit_bytes=24 * 1024 * 1024
         ),

time: 39.7 us -> 39.9 us (level)
  no operation moved by 1% of the time
where the time goes in v6:
time: 39.9 us; the launch traced here: 39.4 us
  Pallas kernels  38.8 us (97%)
  between operations  0.64 us (2%)
    pallas_call x1, Pallas kernels, on_device(): pl.pallas_call(functools.partial(kernel, n_group, n_sub), out_shape=(jax....  37.6 us
    pallas_call x1, Pallas kernels, on_device(): pl.pallas_call(prolong_kernel, out_shape=(jax.ShapeDtypeStruct((2, 2, RHS...  1.17 us

profile of v6, /device:TPU:1, one launch (start us, length us, event | category | flops | bytes accessed | tf_op | source)
XLA Modules:
  0.0 39.4 jit_solution(11405140659999884367)
XLA Ops:
  0.6 37.6 %coarse.1 = (f32[8,128]{1,0:T(8,128)S(1)}, f32[8,128]{1,0:T(8,128)S(1)}, f32[4,1024]{1,0:T(4,128)S(1)}, bf16[2,12,32,1024]{3,2,1,0:T(8,128)(2,1)S(1)}) custom-call(s32[16]{0:T(128)} %owner_ref.1, bf16[2,12,4,1024]{3,2,1,0:T(4,128)(2,1)} %fine_ref.1, bf16[2,12,32,1024]{3,2,1,0:T(8,128)(2,1)} %null_ref.1, s32[1,1024]{1,0:T(1,128)} %agg_ref.1, ...), custom_call_target="tpu_custom_call" | custom-call | tf_op jit(solution)/shard_map/coarse/pallas_call | solution.py:440
  38.3 1.2 %prolong.1 = (f32[2,2,4,64]{3,2,1,0:T(4,128)}, bf16[2,12,4,1024]{3,2,1,0:T(4,128)(2,1)}) custom-call(f32[8,128]{1,0:T(8,128)S(1)} %get-tuple-element.8.sol_ref, f32[8,128]{1,0:T(8,128)S(1)} %get-tuple-element.9.own_ref, f32[4,1024]{1,0:T(4,128)S(1)} %get-tuple-element.10.masks_ref, bf16[2,12,32,1024]{3,2,1,0:T(8,128)(2,1)S(1)} %get-tuple-element.11.null), custom_call_target="tpu_custom_call" | custom-call | tf_op jit(solution)/shard_map/prolong/pallas_call | solution.py:488

commit v7 on v5

--- a/solution.py
+++ b/solution.py
@@ -253,6 +253,13 @@
         for b in range(NBLOCK)
     ]
     load_owner = pltpu.make_async_copy(owner_ref, owner, local_sem.at[3 + NBLOCK])
+    load_agg.start()
+    load_fine.start()
+    for load in load_null:
+        load.start()
+    load_links.start()
+    load_owner.start()
+
     to_t = (0, -1, 1)
     barrier = pltpu.get_barrier_semaphore()
 
@@ -265,13 +272,6 @@
             each(count, lambda i: greet((member(flip, i), device(0, to_t[at])[1])))
     greet(device(0, 2))
     greet(device(0, -2))
-
-    load_agg.start()
-    load_fine.start()
-    for load in load_null:
-        load.start()
-    load_links.start()
-    load_owner.start()
 
     row = lax.broadcasted_iota(jnp.int32, (8, 128), 0)
     lane = lax.broadcasted_iota(jnp.int32, (8, 128), 1)

time: 39.7 us -> 39.6 us (level)
  no operation moved by 1% of the time
where the time goes in v7:
time: 39.6 us; the launch traced here: 39.4 us
  Pallas kernels  38.8 us (98%)
  between operations  0.64 us (2%)
    pallas_call x1, Pallas kernels, on_device(): pl.pallas_call(functools.partial(kernel, n_group, n_sub), out_shape=(jax....  37.6 us
    pallas_call x1, Pallas kernels, on_device(): pl.pallas_call(prolong_kernel, out_shape=(jax.ShapeDtypeStruct((2, 2, RHS...  1.17 us

profile of v7, /device:TPU:1, one launch (start us, length us, event | category | flops | bytes accessed | tf_op | source)
XLA Modules:
  0.0 39.4 jit_solution(3923103912481993005)
XLA Ops:
  0.6 37.6 %coarse.1 = (f32[8,128]{1,0:T(8,128)S(1)}, f32[8,128]{1,0:T(8,128)S(1)}, f32[4,1024]{1,0:T(4,128)S(1)}, bf16[2,12,32,1024]{3,2,1,0:T(8,128)(2,1)S(1)}) custom-call(s32[16]{0:T(128)} %owner_ref.1, bf16[2,12,4,1024]{3,2,1,0:T(4,128)(2,1)} %fine_ref.1, bf16[2,12,32,1024]{3,2,1,0:T(8,128)(2,1)} %null_ref.1, s32[1,1024]{1,0:T(1,128)} %agg_ref.1, ...), custom_call_target="tpu_custom_call" | custom-call | tf_op jit(solution)/shard_map/coarse/pallas_call | solution.py:436
  38.3 1.2 %prolong.1 = (f32[2,2,4,64]{3,2,1,0:T(4,128)}, bf16[2,12,4,1024]{3,2,1,0:T(4,128)(2,1)}) custom-call(f32[8,128]{1,0:T(8,128)S(1)} %get-tuple-element.8.sol_ref, f32[8,128]{1,0:T(8,128)S(1)} %get-tuple-element.9.own_ref, f32[4,1024]{1,0:T(4,128)S(1)} %get-tuple-element.10.masks_ref, bf16[2,12,32,1024]{3,2,1,0:T(8,128)(2,1)S(1)} %get-tuple-element.11.null), custom_call_target="tpu_custom_call" | custom-call | tf_op jit(solution)/shard_map/prolong/pallas_call | solution.py:483
